TPU v7x, 128 devices: a whole 4x4x4 slice. The times are simulated.
128 devices in a mesh: ctx: 8 (over y_lo, x), fsdp: 16 (over z, y_hi, core).
Axes of the slice: x: 4, y: 4 (y_hi: 2, y_lo: 2; y = y_hi * 2 + y_lo), z: 4, core: 2. Of those that a mesh axis runs over, the one named last changes fastest.
Arguments:
- tokens: bfloat16 [16, 2048, 896], P('fsdp', 'ctx'), may hold values from -6 to 6
- cotangent: bfloat16 [16, 2048, 896], P('fsdp', 'ctx'), may hold values from -6 to 6
- layout: int32 [16, 32], P('fsdp'), may hold values from 0 to 31, as said below
- w_query: float32 [896, 896], P(('ctx', 'fsdp')), may hold values from -0.1875 to 0.1875
- m_query: float32 [896, 896], P(('ctx', 'fsdp')), may hold values from -1 to 1
- v_query: float32 [896, 896], P(('ctx', 'fsdp')), may hold values from 0 to 1
- w_key: float32 [896, 128], P(('ctx', 'fsdp')), may hold values from -0.1875 to 0.1875
- m_key: float32 [896, 128], P(('ctx', 'fsdp')), may hold values from -1 to 1
- v_key: float32 [896, 128], P(('ctx', 'fsdp')), may hold values from 0 to 1
- w_value: float32 [896, 128], P(('ctx', 'fsdp')), may hold values from -0.1875 to 0.1875
- m_value: float32 [896, 128], P(('ctx', 'fsdp')), may hold values from -1 to 1
- v_value: float32 [896, 128], P(('ctx', 'fsdp')), may hold values from 0 to 1
- w_out: float32 [896, 896], P(('ctx', 'fsdp')), may hold values from -1 to 1
- m_out: float32 [896, 896], P(('ctx', 'fsdp')), may hold values from -1 to 1
- v_out: float32 [896, 896], P(('ctx', 'fsdp')), may hold values from 0 to 1
- w_gate: float32 [896, 4864], P(('ctx', 'fsdp')), may hold values from -0.1875 to 0.1875
- m_gate: float32 [896, 4864], P(('ctx', 'fsdp')), may hold values from -1 to 1
- v_gate: float32 [896, 4864], P(('ctx', 'fsdp')), may hold values from 0 to 1
- w_up: float32 [896, 4864], P(('ctx', 'fsdp')), may hold values from -0.1875 to 0.1875
- m_up: float32 [896, 4864], P(('ctx', 'fsdp')), may hold values from -1 to 1
- v_up: float32 [896, 4864], P(('ctx', 'fsdp')), may hold values from 0 to 1
- w_down: float32 [896, 4864], P(('ctx', 'fsdp')), may hold values from -0.078125 to 0.078125
- m_down: float32 [896, 4864], P(('ctx', 'fsdp')), may hold values from -1 to 1
- v_down: float32 [896, 4864], P(('ctx', 'fsdp')), may hold values from 0 to 1
- w_vectors: float32 [2944], P(('ctx', 'fsdp')), may hold values from -1 to 4
- m_vectors: float32 [2944], P(('ctx', 'fsdp')), may hold values from -1 to 1
- v_vectors: float32 [2944], P(('ctx', 'fsdp')), may hold values from 0 to 1
Outputs:
- output: bfloat16 [16, 2048, 896], P('fsdp', 'ctx')
- input_grad: float32 [16, 2048, 896], P('fsdp', 'ctx')
- grad_norm: float32 [], replicated
- w_query_new: float32 [896, 896], P(('ctx', 'fsdp'))
- m_query_new: float32 [896, 896], P(('ctx', 'fsdp'))
- v_query_new: float32 [896, 896], P(('ctx', 'fsdp'))
- w_query_copy: bfloat16 [896, 896], P(('ctx', 'fsdp'))
- w_key_new: float32 [896, 128], P(('ctx', 'fsdp'))
- m_key_new: float32 [896, 128], P(('ctx', 'fsdp'))
- v_key_new: float32 [896, 128], P(('ctx', 'fsdp'))
- w_key_copy: bfloat16 [896, 128], P(('ctx', 'fsdp'))
- w_value_new: float32 [896, 128], P(('ctx', 'fsdp'))
- m_value_new: float32 [896, 128], P(('ctx', 'fsdp'))
- v_value_new: float32 [896, 128], P(('ctx', 'fsdp'))
- w_value_copy: bfloat16 [896, 128], P(('ctx', 'fsdp'))
- w_out_new: float32 [896, 896], P(('ctx', 'fsdp'))
- m_out_new: float32 [896, 896], P(('ctx', 'fsdp'))
- v_out_new: float32 [896, 896], P(('ctx', 'fsdp'))
- w_out_copy: bfloat16 [896, 896], P(('ctx', 'fsdp'))
- w_gate_new: float32 [896, 4864], P(('ctx', 'fsdp'))
- m_gate_new: float32 [896, 4864], P(('ctx', 'fsdp'))
- v_gate_new: float32 [896, 4864], P(('ctx', 'fsdp'))
- w_gate_copy: bfloat16 [896, 4864], P(('ctx', 'fsdp'))
- w_up_new: float32 [896, 4864], P(('ctx', 'fsdp'))
- m_up_new: float32 [896, 4864], P(('ctx', 'fsdp'))
- v_up_new: float32 [896, 4864], P(('ctx', 'fsdp'))
- w_up_copy: bfloat16 [896, 4864], P(('ctx', 'fsdp'))
- w_down_new: float32 [896, 4864], P(('ctx', 'fsdp'))
- m_down_new: float32 [896, 4864], P(('ctx', 'fsdp'))
- v_down_new: float32 [896, 4864], P(('ctx', 'fsdp'))
- w_down_copy: bfloat16 [896, 4864], P(('ctx', 'fsdp'))
- w_vectors_new: float32 [2944], P(('ctx', 'fsdp'))
- m_vectors_new: float32 [2944], P(('ctx', 'fsdp'))
- v_vectors_new: float32 [2944], P(('ctx', 'fsdp'))
- w_vectors_copy: bfloat16 [2944], P(('ctx', 'fsdp'))
Inputs may be any that keep to these rules, and one draw needn't show every extreme that they name: `layout`: each row orders all 32 pieces of its group, each once.
All inputs are finite; a program needn't handle non-finite values.
Results may differ from a plain program's by a relative error of at most 0.03.
Values may be sent and summed in bfloat16 or wider, within the bound.
A program may use at most 192 MiB of HBM per device.

v0:
```python
import jax
import jax.numpy as jnp
from jax import lax
from jax.sharding import PartitionSpec as P

HEADS = 14
KV_HEADS = 2
HD = 64
PROMPT = 1024
CONT = 512
PIECE = 64
KBLK = 512
STEP = 10


EPS_NORM = 1e-06
THETA = 1000000.0
CLIP = 1.0
BETA_ONE = 0.9
BETA_TWO = 0.95
ADAM_EPS = 1e-08
STEP_RATES = (0.02, 0.02, 0.02, 0.2, 0.02, 0.02, 0.02, 0.5)
DECAY = 0.1
MASKED = -1e30


def token_tables(layout):
    slot_piece = jnp.repeat(layout, PIECE, axis=1)
    offsets = jnp.tile(jnp.arange(PIECE, dtype=jnp.int32), layout.shape[1])
    prompt_pieces = PROMPT // PIECE
    per_cont = CONT // PIECE
    later = slot_piece - prompt_pieces
    in_prompt = slot_piece < prompt_pieces
    seq_ids = jnp.where(in_prompt, 0, later // per_cont + 1)
    places = (
        jnp.where(in_prompt, slot_piece * PIECE, PROMPT + later % per_cont * PIECE)
        + offsets[None, :]
    )
    return (seq_ids, places)


def rms_norm(row_data, gain_vec):
    return (
        row_data
        * lax.rsqrt(jnp.mean(row_data * row_data, axis=-1, keepdims=True) + EPS_NORM)
        * gain_vec
    )


def swiglu(gate_in, up_in):
    return jax.nn.silu(gate_in) * up_in


def rotate(values, places):
    half_dim = HD // 2
    frequency = THETA ** (-(jnp.arange(half_dim, dtype=jnp.float32) * (2.0 / HD)))
    angles = places.astype(jnp.float32)[..., None] * frequency
    cosine = jnp.cos(angles)[..., None, :]
    sine_part = jnp.sin(angles)[..., None, :]
    front_half = values[..., :half_dim]
    back_half = values[..., half_dim:]
    return jnp.concatenate(
        [front_half * cosine - back_half * sine_part, back_half * cosine + front_half * sine_part],
        axis=-1,
    )


def forward_product(left, right):
    return jnp.dot(left, right, preferred_element_type=jnp.float32)


def outer_sum(left, right):
    return lax.dot_general(
        left, right, (((0,), (0,)), ((), ())), preferred_element_type=jnp.float32
    )


def back_product(gradient, weight):
    return lax.dot_general(
        gradient, weight, (((1,), (1,)), ((), ())), preferred_element_type=jnp.float32
    )


def block_pieces(keys_all, values_all, seq_all, pos_all, block_index):
    start_at = block_index * KBLK
    return (
        lax.dynamic_slice_in_dim(keys_all, start_at, KBLK, 1),
        lax.dynamic_slice_in_dim(values_all, start_at, KBLK, 1),
        lax.dynamic_slice_in_dim(seq_all, start_at, KBLK, 1),
        lax.dynamic_slice_in_dim(pos_all, start_at, KBLK, 1),
    )


def block_scores(query_grp, key_block, seq_query, pos_query, seq_key, pos_key):
    group_count = key_block.shape[0]
    key_heads = key_block.reshape(group_count, KBLK, KV_HEADS, HD)
    scores = jnp.einsum(
        "bqgrd,bkgd->bgrqk", query_grp, key_heads, preferred_element_type=jnp.float32
    ) * HD ** (-0.5)
    allowed = (pos_key[:, None, :] <= pos_query[:, :, None]) & (
        (seq_key[:, None, :] == 0) | (seq_key[:, None, :] == seq_query[:, :, None])
    )
    return (scores, allowed[:, None, None], key_heads)


def to_rows(values):
    return jnp.transpose(values, (0, 3, 1, 2))[..., None]


def attend(query_grp, keys_all, values_all, seq_query, pos_query, seq_all, pos_all):
    group_count, query_count = (query_grp.shape[0], query_grp.shape[1])
    repeat = query_grp.shape[3]
    blocks = keys_all.shape[1] // KBLK

    def advance(carried, block_index):
        top_score, sum_exp, running = carried
        key_block, value_block, seq_key, pos_key = block_pieces(
            keys_all, values_all, seq_all, pos_all, block_index
        )
        scores, allowed, key_heads = block_scores(
            query_grp, key_block, seq_query, pos_query, seq_key, pos_key
        )
        masked = jnp.where(allowed, scores, MASKED)
        new_top = jnp.maximum(top_score, jnp.max(masked, axis=-1))
        scale_old = jnp.exp(top_score - new_top)
        weights = jnp.where(allowed, jnp.exp(masked - new_top[..., None]), 0.0)
        sum_exp = sum_exp * scale_old + jnp.sum(weights, axis=-1)
        value_heads = value_block.reshape(key_block.shape[0], KBLK, KV_HEADS, HD)
        update = jnp.einsum(
            "bgrqk,bkgd->bqgrd",
            weights.astype(jnp.bfloat16),
            value_heads,
            preferred_element_type=jnp.float32,
        )
        running = running * to_rows(scale_old) + update
        return ((new_top, sum_exp, running), None)

    start_top = jnp.full((group_count, KV_HEADS, repeat, query_count), MASKED, jnp.float32)
    start_sum = jnp.zeros((group_count, KV_HEADS, repeat, query_count), jnp.float32)
    start_run = jnp.zeros(query_grp.shape, jnp.float32)
    (top_score, sum_exp, running), ignored = lax.scan(
        advance, (start_top, start_sum, start_run), jnp.arange(blocks, dtype=jnp.int32)
    )
    return (running / to_rows(sum_exp), top_score + jnp.log(sum_exp))


def block_probabilities(
    query_grp, keys_all, values_all, seq_query, pos_query, seq_all, pos_all, log_total, block_index
):
    key_block, value_block, seq_key, pos_key = block_pieces(
        keys_all, values_all, seq_all, pos_all, block_index
    )
    scores, allowed, key_heads = block_scores(
        query_grp, key_block, seq_query, pos_query, seq_key, pos_key
    )
    masked = jnp.where(allowed, scores, MASKED)
    probabilities = jnp.where(allowed, jnp.exp(masked - log_total[..., None]), 0.0)
    value_heads = value_block.reshape(key_block.shape[0], KBLK, KV_HEADS, HD)
    return (probabilities, key_heads, value_heads)


def attend_back(
    query_grp,
    grad_grp,
    keys_all,
    values_all,
    seq_query,
    pos_query,
    seq_all,
    pos_all,
    log_total,
    row_terms,
):
    blocks = keys_all.shape[1] // KBLK
    group_count = keys_all.shape[0]
    score_scale = HD ** (-0.5)

    def second_pass(running, block_index):
        probabilities, key_heads, value_heads = block_probabilities(
            query_grp,
            keys_all,
            values_all,
            seq_query,
            pos_query,
            seq_all,
            pos_all,
            log_total,
            block_index,
        )
        grad_probs = jnp.einsum(
            "bqgrd,bkgd->bgrqk", grad_grp, value_heads, preferred_element_type=jnp.float32
        )
        grad_scores = (probabilities * (grad_probs - row_terms[..., None])).astype(jnp.bfloat16)
        running = (
            running
            + jnp.einsum(
                "bgrqk,bkgd->bqgrd", grad_scores, key_heads, preferred_element_type=jnp.float32
            )
            * score_scale
        )
        key_grad = (
            jnp.einsum(
                "bgrqk,bqgrd->bkgd", grad_scores, query_grp, preferred_element_type=jnp.float32
            )
            * score_scale
        )
        value_grad = jnp.einsum(
            "bgrqk,bqgrd->bkgd",
            probabilities.astype(jnp.bfloat16),
            grad_grp,
            preferred_element_type=jnp.float32,
        )
        return (running, (key_grad, value_grad))

    grad_query, (key_blocks, value_blocks) = lax.scan(
        second_pass, jnp.zeros(query_grp.shape, jnp.float32), jnp.arange(blocks, dtype=jnp.int32)
    )
    kv_width = KV_HEADS * HD
    key_grads = jnp.moveaxis(key_blocks, 0, 1).reshape(group_count, blocks * KBLK, kv_width)
    value_grads = jnp.moveaxis(value_blocks, 0, 1).reshape(group_count, blocks * KBLK, kv_width)
    return (grad_query, key_grads, value_grads)


def adam_step(master, first_moment, second_moment, gradient, factor, step_rate, weight_decay):
    clipped = gradient * factor
    first_new = BETA_ONE * first_moment + (1.0 - BETA_ONE) * clipped
    second_new = BETA_TWO * second_moment + (1.0 - BETA_TWO) * clipped * clipped
    direction = (
        first_new
        / (1.0 - BETA_ONE**STEP)
        / (jnp.sqrt(second_new / (1.0 - BETA_TWO**STEP)) + ADAM_EPS)
    )
    master_new = master - step_rate * (direction + weight_decay * master)
    return (master_new, first_new, second_new, master_new.astype(jnp.bfloat16))


def per_device(
    tokens,
    cotangent,
    layout,
    w_query,
    m_query,
    v_query,
    w_key,
    m_key,
    v_key,
    w_value,
    m_value,
    v_value,
    w_out,
    m_out,
    v_out,
    w_gate,
    m_gate,
    v_gate,
    w_up,
    m_up,
    v_up,
    w_down,
    m_down,
    v_down,
    w_vectors,
    m_vectors,
    v_vectors,
):
    group_count, tok_dev, model_width = tokens.shape
    row_count = group_count * tok_dev
    query_width = HEADS * HD
    kv_width = KV_HEADS * HD
    repeat = HEADS // KV_HEADS
    seq_all, pos_all = token_tables(layout)
    start_at = lax.axis_index("ctx") * tok_dev
    seq_mine = lax.dynamic_slice_in_dim(seq_all, start_at, tok_dev, 1)
    pos_mine = lax.dynamic_slice_in_dim(pos_all, start_at, tok_dev, 1)
    query_full, key_full, value_full, out_full, vector_full = (
        lax.all_gather(w_query.astype(jnp.bfloat16), ("ctx", "fsdp"), axis=0, tiled=True),
        lax.all_gather(w_key.astype(jnp.bfloat16), ("ctx", "fsdp"), axis=0, tiled=True),
        lax.all_gather(w_value.astype(jnp.bfloat16), ("ctx", "fsdp"), axis=0, tiled=True),
        lax.all_gather(w_out.astype(jnp.bfloat16), ("ctx", "fsdp"), axis=0, tiled=True),
        lax.all_gather(w_vectors.astype(jnp.bfloat16), ("ctx", "fsdp"), axis=0, tiled=True),
    )
    vector_float = vector_full.astype(jnp.float32)
    gain_attn = vector_float[:model_width]
    gain_mlp = vector_float[model_width : 2 * model_width]
    bias_query = vector_float[2 * model_width : 2 * model_width + query_width]
    bias_key = vector_float[
        2 * model_width + query_width : 2 * model_width + query_width + kv_width
    ]
    bias_value = vector_float[2 * model_width + query_width + kv_width :]
    inputs = tokens.reshape(row_count, model_width).astype(jnp.float32)
    normed_one, norm_one_back = jax.vjp(rms_norm, inputs, gain_attn)
    normed_one = normed_one.astype(jnp.bfloat16)
    query_pre = forward_product(normed_one, query_full) + bias_query
    key_pre = forward_product(normed_one, key_full) + bias_key
    value_pre = forward_product(normed_one, value_full) + bias_value
    query_rot = rotate(query_pre.reshape(group_count, tok_dev, HEADS, HD), pos_mine).astype(
        jnp.bfloat16
    )
    query_grp = query_rot.reshape(group_count, tok_dev, KV_HEADS, repeat, HD)
    key_rot = (
        rotate(key_pre.reshape(group_count, tok_dev, KV_HEADS, HD), pos_mine)
        .astype(jnp.bfloat16)
        .reshape(group_count, tok_dev, kv_width)
    )
    value_low = value_pre.astype(jnp.bfloat16).reshape(group_count, tok_dev, kv_width)
    keys_all, values_all = (
        lax.all_gather(key_rot, "ctx", axis=1, tiled=True),
        lax.all_gather(value_low, "ctx", axis=1, tiled=True),
    )
    attended_float, log_total = attend(
        query_grp, keys_all, values_all, seq_mine, pos_mine, seq_all, pos_all
    )
    attended = attended_float.reshape(row_count, query_width).astype(jnp.bfloat16)
    mixed = inputs + forward_product(attended, out_full)
    gate_full, up_full, down_full = (
        lax.all_gather(w_gate.astype(jnp.bfloat16), ("ctx", "fsdp"), axis=0, tiled=True),
        lax.all_gather(w_up.astype(jnp.bfloat16), ("ctx", "fsdp"), axis=0, tiled=True),
        lax.all_gather(w_down.astype(jnp.bfloat16), ("ctx", "fsdp"), axis=0, tiled=True),
    )
    normed_two, norm_two_back = jax.vjp(rms_norm, mixed, gain_mlp)
    normed_two = normed_two.astype(jnp.bfloat16)
    gate_pre = forward_product(normed_two, gate_full)
    up_pre = forward_product(normed_two, up_full)
    hidden, hidden_back = jax.vjp(swiglu, gate_pre, up_pre)
    hidden = hidden.astype(jnp.bfloat16)
    result = mixed + back_product(hidden, down_full)
    output = result.astype(jnp.bfloat16).reshape(group_count, tok_dev, model_width)
    gate_back, up_back, down_back = (
        lax.all_gather(w_gate.astype(jnp.bfloat16), ("ctx", "fsdp"), axis=0, tiled=True),
        lax.all_gather(w_up.astype(jnp.bfloat16), ("ctx", "fsdp"), axis=0, tiled=True),
        lax.all_gather(w_down.astype(jnp.bfloat16), ("ctx", "fsdp"), axis=0, tiled=True),
    )
    grad_output = cotangent.reshape(row_count, model_width)
    grad_hidden = forward_product(grad_output, down_back)
    grad_wdown = outer_sum(grad_output, hidden)
    grad_gate, grad_up = hidden_back(grad_hidden)
    grad_gate = grad_gate.astype(jnp.bfloat16)
    grad_up = grad_up.astype(jnp.bfloat16)
    grad_wgate = outer_sum(normed_two, grad_gate)
    grad_wup = outer_sum(normed_two, grad_up)
    grad_norm_two = back_product(grad_gate, gate_back) + back_product(grad_up, up_back)
    grad_mixed_part, grad_gain_mlp = norm_two_back(grad_norm_two)
    grad_mixed = grad_output.astype(jnp.float32) + grad_mixed_part
    grad_branch = grad_mixed.astype(jnp.bfloat16)
    query_back, key_back, value_back, out_back = (
        lax.all_gather(w_query.astype(jnp.bfloat16), ("ctx", "fsdp"), axis=0, tiled=True),
        lax.all_gather(w_key.astype(jnp.bfloat16), ("ctx", "fsdp"), axis=0, tiled=True),
        lax.all_gather(w_value.astype(jnp.bfloat16), ("ctx", "fsdp"), axis=0, tiled=True),
        lax.all_gather(w_out.astype(jnp.bfloat16), ("ctx", "fsdp"), axis=0, tiled=True),
    )
    grad_wout = outer_sum(attended, grad_branch)
    grad_attended = back_product(grad_branch, out_back).astype(jnp.bfloat16)
    grad_attended = grad_attended.reshape(group_count, tok_dev, KV_HEADS, repeat, HD)
    row_terms = jnp.einsum("bqgrd,bqgrd->bgrq", grad_attended.astype(jnp.float32), attended_float)
    keys_back, values_back = (keys_all, values_all)
    grad_query, key_grads, value_grads = attend_back(
        query_grp,
        grad_attended,
        keys_back,
        values_back,
        seq_mine,
        pos_mine,
        seq_all,
        pos_all,
        log_total,
        row_terms,
    )
    key_mine, value_mine = (
        lax.psum_scatter(
            key_grads.astype(jnp.bfloat16), "ctx", scatter_dimension=1, tiled=True
        ).astype(jnp.float32),
        lax.psum_scatter(
            value_grads.astype(jnp.bfloat16), "ctx", scatter_dimension=1, tiled=True
        ).astype(jnp.float32),
    )
    grad_qpre = (
        rotate(grad_query.reshape(group_count, tok_dev, HEADS, HD), -pos_mine)
        .reshape(row_count, query_width)
        .astype(jnp.bfloat16)
    )
    grad_kpre = (
        rotate(key_mine.reshape(group_count, tok_dev, KV_HEADS, HD), -pos_mine)
        .reshape(row_count, kv_width)
        .astype(jnp.bfloat16)
    )
    grad_vpre = value_mine.reshape(row_count, kv_width).astype(jnp.bfloat16)
    grad_wquery = outer_sum(normed_one, grad_qpre)
    grad_wkey = outer_sum(normed_one, grad_kpre)
    grad_wvalue = outer_sum(normed_one, grad_vpre)
    grad_norm_one = (
        back_product(grad_qpre, query_back)
        + back_product(grad_kpre, key_back)
        + back_product(grad_vpre, value_back)
    )
    grad_input_part, grad_gain_attn = norm_one_back(grad_norm_one)
    input_grad = (grad_mixed + grad_input_part).reshape(group_count, tok_dev, model_width)
    grad_vectors = jnp.concatenate(
        [
            grad_gain_attn,
            grad_gain_mlp,
            jnp.sum(grad_qpre.astype(jnp.float32), axis=0),
            jnp.sum(grad_kpre.astype(jnp.float32), axis=0),
            jnp.sum(grad_vpre.astype(jnp.float32), axis=0),
        ]
    )
    shard_query, shard_key, shard_value, shard_out, shard_vectors = (
        lax.psum_scatter(grad_wquery, ("ctx", "fsdp"), scatter_dimension=0, tiled=True),
        lax.psum_scatter(grad_wkey, ("ctx", "fsdp"), scatter_dimension=0, tiled=True),
        lax.psum_scatter(grad_wvalue, ("ctx", "fsdp"), scatter_dimension=0, tiled=True),
        lax.psum_scatter(grad_wout, ("ctx", "fsdp"), scatter_dimension=0, tiled=True),
        lax.psum_scatter(grad_vectors, ("ctx", "fsdp"), scatter_dimension=0, tiled=True),
    )
    shard_gate, shard_up, shard_down = (
        lax.psum_scatter(grad_wgate, ("ctx", "fsdp"), scatter_dimension=0, tiled=True),
        lax.psum_scatter(grad_wup, ("ctx", "fsdp"), scatter_dimension=0, tiled=True),
        lax.psum_scatter(grad_wdown, ("ctx", "fsdp"), scatter_dimension=0, tiled=True),
    )
    shard_grads = (
        shard_query,
        shard_key,
        shard_value,
        shard_out,
        shard_gate,
        shard_up,
        shard_down,
        shard_vectors,
    )
    local_square = jnp.zeros((), jnp.float32)
    for shard_grad in shard_grads:
        local_square = local_square + jnp.sum(shard_grad * shard_grad)
    square_sum = lax.psum(local_square, ("ctx", "fsdp"))
    grad_norm = jnp.sqrt(square_sum)
    factor = CLIP / jnp.maximum(grad_norm, CLIP)
    masters = (w_query, w_key, w_value, w_out, w_gate, w_up, w_down, w_vectors)
    firsts = (m_query, m_key, m_value, m_out, m_gate, m_up, m_down, m_vectors)
    seconds = (v_query, v_key, v_value, v_out, v_gate, v_up, v_down, v_vectors)
    results = [output, input_grad, grad_norm]
    for number in range(8):
        step_rate = STEP_RATES[number]
        weight_decay = 0.0 if number == 7 else DECAY
        results.extend(
            adam_step(
                masters[number],
                firsts[number],
                seconds[number],
                shard_grads[number],
                factor,
                step_rate,
                weight_decay,
            )
        )
    return tuple(results)


def solution(mesh):
    in_specs = (
        P("fsdp", "ctx", None),
        P("fsdp", "ctx", None),
        P("fsdp", None),
        P(("ctx", "fsdp"), None),
        P(("ctx", "fsdp"), None),
        P(("ctx", "fsdp"), None),
        P(("ctx", "fsdp"), None),
        P(("ctx", "fsdp"), None),
        P(("ctx", "fsdp"), None),
        P(("ctx", "fsdp"), None),
        P(("ctx", "fsdp"), None),
        P(("ctx", "fsdp"), None),
        P(("ctx", "fsdp"), None),
        P(("ctx", "fsdp"), None),
        P(("ctx", "fsdp"), None),
        P(("ctx", "fsdp"), None),
        P(("ctx", "fsdp"), None),
        P(("ctx", "fsdp"), None),
        P(("ctx", "fsdp"), None),
        P(("ctx", "fsdp"), None),
        P(("ctx", "fsdp"), None),
        P(("ctx", "fsdp"), None),
        P(("ctx", "fsdp"), None),
        P(("ctx", "fsdp"), None),
        P(("ctx", "fsdp")),
        P(("ctx", "fsdp")),
        P(("ctx", "fsdp")),
    )
    out_specs = (
        P("fsdp", "ctx", None),
        P("fsdp", "ctx", None),
        P(),
        P(("ctx", "fsdp"), None),
        P(("ctx", "fsdp"), None),
        P(("ctx", "fsdp"), None),
        P(("ctx", "fsdp"), None),
        P(("ctx", "fsdp"), None),
        P(("ctx", "fsdp"), None),
        P(("ctx", "fsdp"), None),
        P(("ctx", "fsdp"), None),
        P(("ctx", "fsdp"), None),
        P(("ctx", "fsdp"), None),
        P(("ctx", "fsdp"), None),
        P(("ctx", "fsdp"), None),
        P(("ctx", "fsdp"), None),
        P(("ctx", "fsdp"), None),
        P(("ctx", "fsdp"), None),
        P(("ctx", "fsdp"), None),
        P(("ctx", "fsdp"), None),
        P(("ctx", "fsdp"), None),
        P(("ctx", "fsdp"), None),
        P(("ctx", "fsdp"), None),
        P(("ctx", "fsdp"), None),
        P(("ctx", "fsdp"), None),
        P(("ctx", "fsdp"), None),
        P(("ctx", "fsdp"), None),
        P(("ctx", "fsdp"), None),
        P(("ctx", "fsdp"), None),
        P(("ctx", "fsdp"), None),
        P(("ctx", "fsdp"), None),
        P(("ctx", "fsdp")),
        P(("ctx", "fsdp")),
        P(("ctx", "fsdp")),
        P(("ctx", "fsdp")),
    )
    return jax.shard_map(
        per_device, mesh=mesh, in_specs=in_specs, out_specs=out_specs, check_vma=False
    )
```

profile of v0, /device:TPU:1, one launch (start us, length us, event | category | flops | bytes accessed | tf_op | source)
XLA Modules:
  0.0 2500.3 jit_solution(14306699739466100249)
XLA Ops:
  20.3 180.8 %all-gather.3 = bf16[128,7,128]{2,1,0:T(8,128)(2,1)S(1)} all-gather(bf16[1,7,128]{2,1,0:T(8,128)(2,1)S(1)} %convert_bitcast_fusion.6), channel_id=1, replica_groups=mesh['ctx'=8,'fsdp'=16] {'ctx','fsdp'}, dimensions={0}, use_global_device_ids=true | all-gather | bytes 231168 | tf_op jit(solution)/shard_map/all_gather | solution.py:278
  201.3 171.1 %all-gather.1 = bf16[128,7,128]{2,1,0:T(8,128)(2,1)S(1)} all-gather(bf16[1,7,128]{2,1,0:T(8,128)(2,1)S(1)} %convert_bitcast_fusion.7), channel_id=1, replica_groups=mesh['ctx'=8,'fsdp'=16] {'ctx','fsdp'}, dimensions={0}, use_global_device_ids=true | all-gather | bytes 231168 | tf_op jit(solution)/shard_map/all_gather | solution.py:277
  372.8 62.8 %all-reduce = bf16[2944]{0:T(1024)(128)(2,1)S(1)} all-reduce(bf16[2944]{0:T(1024)(128)(2,1)S(1)} %dynamic-update-slice), channel_id=1, replica_groups=mesh['ctx'=8,'fsdp'=16] {'ctx','fsdp'}, use_global_device_ids=true, to_apply=%add | all-reduce | flops 2944 | bytes 11776
  437.0 23.3 all-gather
  462.7 25.6 %all_gather.39 = bf16[1,2048,128]{1,2,0:T(8,128)(2,1)} all-gather(bf16[1,256,128]{1,2,0:T(8,128)(2,1)S(1)} %bitcast.438), channel_id=1, replica_groups=mesh['ctx'=8,'fsdp'=16] {'ctx'}, dimensions={1}, use_global_device_ids=true | all-gather | bytes 589824 | tf_op jit(solution)/shard_map/all_gather | solution.py:307
  499.5 34.4 %while.30 = (s32[]{:T(128)}, f32[1,2,7,256]{3,2,1,0:T(8,128)S(1)}, f32[1,2,7,256]{3,2,1,0:T(8,128)S(1)}, f32[1,256,2,7,64]{1,4,3,2,0:T(8,128)}, s32[4]{0:T(128)S...) while((s32[]{:T(128)}, f32[1,2,7,256]{3,2,1,0:T(8,128)S(1)}, ...), condition=%wide.region_4.5_spmd.clone, body=%wide.region_1.4_spmd.clone.sunk | while | flops 494851584 | bytes 33211680 | solution.py:141
  537.1 73.5 %all-gather.18.cloned.1.call-done = bf16[128,7,4864]{2,1,0:T(8,128)(2,1)} async-done(((bf16[1,7,4864]{2,1,0:T(8,128)(2,1)}), bf16[128,7,4864]{2,1,0:T(8,128)(2,1)}) %all-gather.18.cloned.1.call-update) | async-done | bytes 8716304 | tf_op jit(solution)/shard_map/all_gather | solution.py:316
  610.7 13.5 reshape.1067
  624.2 193.5 %all-gather.20.cloned.1.call-done = bf16[128,7,4864]{2,1,0:T(8,128)(2,1)} async-done(((bf16[1,7,4864]{2,1,0:T(8,128)(2,1)}), bf16[128,7,4864]{2,1,0:T(8,128)(2,1)}) %all-gather.20.cloned.1.call-update) | async-done | bytes 8716304 | tf_op jit(solution)/shard_map/all_gather | solution.py:317
  817.7 13.5 reshape.1069
  831.2 8.1 fusion.128
  843.6 180.9 %all-gather.22.cloned.1.call-done = bf16[128,7,4864]{2,1,0:T(8,128)(2,1)} async-done(((bf16[1,7,4864]{2,1,0:T(8,128)(2,1)}), bf16[128,7,4864]{2,1,0:T(8,128)(2,1)}) %all-gather.22.cloned.1.call-update) | async-done | bytes 8716304 | tf_op jit(solution)/shard_map/all_gather | solution.py:318
  1024.5 13.5 reshape.1071
  1038.0 10.7 multiply_convert_fusion
  1050.2 7.5 convolution_bitcast_fusion.1
  1057.8 18.9 copy.99
  1076.7 371.9 %fusion.2 = f32[8,4864]{1,0:T(8,128)S(1)} fusion(f32[896,4864]{1,0:T(8,128)} %copy.99), kind=kCustom, calls=%all-reduce-scatter.2 | all-reduce-scatter fusion | flops 4980737 | bytes 17588224
  1453.1 7.1 fusion.129
  1460.3 8.5 fusion.132
  1476.9 42.9 %while.31 = (s32[]{:T(128)}, f32[1,256,2,7,64]{1,4,3,2,0:T(8,128)S(1)}, bf16[4,1,512,2,64]{2,4,3,1,0:T(8,128)(2,1)}, bf16[4,1,512,2,64]{2,4,3,1,0:T(8,128)(2,1)}...) while((s32[]{:T(128)}, ...), condition=%wide.region_8.9_spmd.clone, body=%wide.region_7.8_spmd.clone.sunk | while | flops 1197703680 | bytes 46986616 | solution.py:215
  1530.2 8.5 fusion.131
  1538.8 449.8 %fusion.108 = (f32[8,4864]{1,0:T(8,128)S(1)}, f32[8,4864]{1,0:T(8,128)S(1)}) fusion(f32[896,4864]{1,0:T(8,128)} %fusion.131, f32[896,4864]{1,0:T(8,128)} %fusion.132), kind=kCustom, calls=%all-reduce-scatter.3 | all-reduce-scatter fusion | flops 9961473 | bytes 35176448
  2021.6 11.5 collective-permute-start.36
  2039.2 9.9 collective-permute-start.32
  2083.4 11.0 collective-permute-start.5
  2130.1 7.0 collective-permute-start.24
  2146.4 7.8 fusion.57
  2176.6 52.3 %concatenate.59 = f32[135,4864]{1,0:T(8,128)} concatenate(f32[7,4864]{1,0:T(8,128)} %collective-permute-done.47, f32[8,4864]{1,0:T(8,128)} %collective-permute-done.46, f32[8,4864]{1,0:T(8,128)} %collective-permute-done.45, f32[8,4864]{1,0:T(8,128)} %collective-permute-done.44, f32[8,4864]{1,0:T(8,128)} %collective-permute-done.43, f32[8,4864]{1,0:T(8,128)} %collective-permute-done.42, ...), dimensions={0} | concatenate | bytes 5253120
  2228.8 52.2 %concatenate.57 = f32[135,4864]{1,0:T(8,128)} concatenate(f32[7,4864]{1,0:T(8,128)} %collective-permute-done.15, f32[8,4864]{1,0:T(8,128)} %copy-done.41, f32[8,4864]{1,0:T(8,128)} %copy-done.42, f32[8,4864]{1,0:T(8,128)} %copy-done.43, f32[8,4864]{1,0:T(8,128)} %copy-done.44, f32[8,4864]{1,0:T(8,128)} %copy-done.45, f32[8,4864]{1,0:T(8,128)} %copy-done.46, ...), dimensions={0} | concatenate | bytes 5253120
  2281.0 52.3 %concatenate.58 = f32[135,4864]{1,0:T(8,128)} concatenate(f32[7,4864]{1,0:T(8,128)} %collective-permute-done.31, f32[8,4864]{1,0:T(8,128)} %collective-permute-done.30, f32[8,4864]{1,0:T(8,128)} %collective-permute-done.29, f32[8,4864]{1,0:T(8,128)} %collective-permute-done.28, f32[8,4864]{1,0:T(8,128)} %collective-permute-done.27, f32[8,4864]{1,0:T(8,128)} %collective-permute-done.26, ...), dimensions={0} | concatenate | bytes 5253120
  2341.3 63.0 %all-reduce.8 = f32[2944]{0:T(1024)S(1)} all-reduce(f32[2944]{0:T(1024)S(1)} %constant_dynamic-update-slice_fusion), channel_id=12, replica_groups=mesh['ctx'=8,'fsdp'=16] {'ctx','fsdp'}, use_global_device_ids=true, to_apply=%region_31.32.clone | all-reduce | flops 2944 | bytes 23552
  2415.6 63.7 %psum.7 = f32[]{:T(128)} all-reduce(f32[]{:T(128)S(6)} %add.363), channel_id=1, replica_groups=mesh['ctx'=8,'fsdp'=16] {'ctx','fsdp'}, use_global_device_ids=true, to_apply=%region_33.34 | all-reduce | flops 1 | bytes 8 | tf_op jit(solution)/shard_map/psum | solution.py:431
  (498 shorter events, 297.2 us)
Async XLA Ops:
  7.2 481.0 %all-gather.14.cloned.1.call-start = ((), (), s32[]{:S(2)}) async-start(), calls=%async_computation.4 | async-start | bytes 1849344 | tf_op jit(solution)/shard_map/all_gather | solution.py:276
  8.7 486.3 %all-gather.16.cloned.1.call-start = ((), (), s32[]{:S(2)}) async-start(), calls=%async_computation.5 | async-start | bytes 1849344 | tf_op jit(solution)/shard_map/all_gather | solution.py:279
  10.1 600.6 %all-gather.18.cloned.1.call-start = ((), (), s32[]{:S(2)}) async-start(), calls=%async_computation.6 | async-start | bytes 10039296 | tf_op jit(solution)/shard_map/all_gather | solution.py:316
  11.8 805.9 %all-gather.20.cloned.1.call-start = ((), (), s32[]{:S(2)}) async-start(), calls=%async_computation.7 | async-start | bytes 10039296 | tf_op jit(solution)/shard_map/all_gather | solution.py:317
  13.4 1011.2 %all-gather.22.cloned.1.call-start = ((), (), s32[]{:S(2)}) async-start(), calls=%async_computation.8 | async-start | bytes 10039296 | tf_op jit(solution)/shard_map/all_gather | solution.py:318
  15.0 1981.5 %reduce-scatter.9.cloned.1.call-start = ((), (), s32[]{:S(2)}) async-start(), calls=%async_computation.2 | async-start | bytes 589824 | tf_op jit(solution)/shard_map/reduce_scatter | solution.py:369
  1449.2 558.1 %collective-permute-start.46 = (f32[8,4864]{1,0:T(8,128)S(1)}, f32[8,4864]{1,0:T(8,128)}, u32[]{:S(2)}, u32[]{:S(2)}) collective-permute-start(f32[8,4864]{1,0:T(8,128)S(1)} %fusion.2), channel_id=1, source_target_pairs={{0,15},{1,16},{2,17},{3,18},{4,19},{5,20},{6,21},{7,22},{8,23},{9,... | collective-permute-start | bytes 466952
  1451.2 557.4 %collective-permute-start.45 = (f32[8,4864]{1,0:T(8,128)S(1)}, f32[8,4864]{1,0:T(8,128)}, u32[]{:S(2)}, u32[]{:S(2)}) collective-permute-start(f32[8,4864]{1,0:T(8,128)S(1)} %fusion.2), channel_id=1, source_target_pairs={{0,14},{1,15},{2,16},{3,17},{4,18},{5,19},{6,20},{7,21},{8,22},{9,... | collective-permute-start | bytes 466952
  1525.2 480.0 %reduce-scatter.11.cloned.1.call-start = ((), (), s32[]{:S(2)}) async-start(), calls=%async_computation.3 | async-start | bytes 589824 | tf_op jit(solution)/shard_map/reduce_scatter | solution.py:372
  1525.2 474.1 %collective-permute-start.47 = (f32[7,4864]{1,0:T(8,128)}, f32[7,4864]{1,0:T(8,128)}, u32[]{:S(2)}, u32[]{:S(2)}) collective-permute-start(f32[7,4864]{1,0:T(8,128)} %slice.67), channel_id=1, source_target_pairs={{0,16},{1,17},{2,18},{3,19},{4,20},{5,21},{6,22},{7,23},{8,24},{9,... | collective-permute-start | bytes 408584
  1538.7 866.3 %all-reduce.16.cloned.1.call-start = ((), (), s32[]{:S(2)}) async-start(), calls=%async_computation.9 | async-start | bytes 14680064
  2008.6 24.4 collective-permute-start.40
  2009.9 24.4 collective-permute-start.39
  2021.6 27.6 %collective-permute-start.36 = (f32[8,4864]{1,0:T(8,128)S(1)}, f32[8,4864]{1,0:T(8,128)S(1)}, u32[]{:S(2)}, u32[]{:S(2)}) collective-permute-start(f32[8,4864]{1,0:T(8,128)S(1)} %fusion.2), channel_id=1, source_target_pairs={{0,5},{1,6},{2,7},{3,8},{4,9},{5,10},{6,11},{7,12},{8,13},{9,14},{... | collective-permute-start | bytes 466952
  2034.4 23.5 collective-permute-start.34
  2035.7 25.6 %collective-permute-start.33 = (f32[8,4864]{1,0:T(8,128)S(1)}, f32[8,4864]{1,0:T(8,128)S(1)}, u32[]{:S(2)}, u32[]{:S(2)}) collective-permute-start(f32[8,4864]{1,0:T(8,128)S(1)} %fusion.2), channel_id=1, source_target_pairs={{0,2},{1,3},{2,4},{3,5},{4,6},{5,7},{6,8},{7,9},{8,10},{9,11},{10,... | collective-permute-start | bytes 466952
  2039.2 24.0 collective-permute-start.32
  2064.6 29.8 %collective-permute-start.9 = (f32[8,4864]{1,0:T(8,128)S(1)}, f32[8,4864]{1,0:T(8,128)S(1)}, u32[]{:S(2)}, u32[]{:S(2)}) collective-permute-start(f32[8,4864]{1,0:T(8,128)S(1)} %get-tuple-element.416), channel_id=1, source_target_pairs={{0,10},{1,11},{2,12},{3,13},{4,14},{5,15},{6,16},{7,17},{8,18},{9,... | collective-permute-start | bytes 466952
  2067.8 28.0 %collective-permute-start.8 = (f32[8,4864]{1,0:T(8,128)S(1)}, f32[8,4864]{1,0:T(8,128)S(1)}, u32[]{:S(2)}, u32[]{:S(2)}) collective-permute-start(f32[8,4864]{1,0:T(8,128)S(1)} %get-tuple-element.416), channel_id=1, source_target_pairs={{0,9},{1,10},{2,11},{3,12},{4,13},{5,14},{6,15},{7,16},{8,17},{9,1... | collective-permute-start | bytes 466952
  2074.7 22.4 collective-permute-start.7
  2077.2 23.9 collective-permute-start.6
  2120.5 21.9 collective-permute-start.27
  2125.4 28.9 %collective-permute-start.25 = (f32[8,4864]{1,0:T(8,128)S(1)}, f32[8,4864]{1,0:T(8,128)}, u32[]{:S(2)}, u32[]{:S(2)}) collective-permute-start(f32[8,4864]{1,0:T(8,128)S(1)} %get-tuple-element.417), channel_id=1, source_target_pairs={{0,10},{1,11},{2,12},{3,13},{4,14},{5,15},{6,16},{7,17},{8,18},{9,... | collective-permute-start | bytes 466952
  2130.1 30.8 %collective-permute-start.24 = (f32[8,4864]{1,0:T(8,128)S(1)}, f32[8,4864]{1,0:T(8,128)}, u32[]{:S(2)}, u32[]{:S(2)}) collective-permute-start(f32[8,4864]{1,0:T(8,128)S(1)} %get-tuple-element.417), channel_id=1, source_target_pairs={{0,9},{1,10},{2,11},{3,12},{4,13},{5,14},{6,15},{7,16},{8,17},{9,1... | collective-permute-start | bytes 466952
  2137.1 26.8 %collective-permute-start.23 = (f32[8,4864]{1,0:T(8,128)S(1)}, f32[8,4864]{1,0:T(8,128)}, u32[]{:S(2)}, u32[]{:S(2)}) collective-permute-start(f32[8,4864]{1,0:T(8,128)S(1)} %get-tuple-element.417), channel_id=1, source_target_pairs={{0,8},{1,9},{2,10},{3,11},{4,12},{5,13},{6,14},{7,15},{8,16},{9,17... | collective-permute-start | bytes 466952
  2142.5 23.4 collective-permute-start.22
  2144.4 26.1 %collective-permute-start.21 = (f32[8,4864]{1,0:T(8,128)S(1)}, f32[8,4864]{1,0:T(8,128)}, u32[]{:S(2)}, u32[]{:S(2)}) collective-permute-start(f32[8,4864]{1,0:T(8,128)S(1)} %get-tuple-element.417), channel_id=1, source_target_pairs={{0,6},{1,7},{2,8},{3,9},{4,10},{5,11},{6,12},{7,13},{8,14},{9,15},... | collective-permute-start | bytes 466952
  2154.2 126.8 %collective-permute-start.20 = (f32[8,4864]{1,0:T(8,128)S(1)}, f32[8,4864]{1,0:T(8,128)}, u32[]{:S(2)}, u32[]{:S(2)}) collective-permute-start(f32[8,4864]{1,0:T(8,128)S(1)} %get-tuple-element.417), channel_id=1, source_target_pairs={{0,5},{1,6},{2,7},{3,8},{4,9},{5,10},{6,11},{7,12},{8,13},{9,14},{... | collective-permute-start | bytes 466952
  2160.9 120.1 %collective-permute-start.19 = (f32[8,4864]{1,0:T(8,128)S(1)}, f32[8,4864]{1,0:T(8,128)}, u32[]{:S(2)}, u32[]{:S(2)}) collective-permute-start(f32[8,4864]{1,0:T(8,128)S(1)} %get-tuple-element.417), channel_id=1, source_target_pairs={{0,4},{1,5},{2,6},{3,7},{4,8},{5,9},{6,10},{7,11},{8,12},{9,13},{1... | collective-permute-start | bytes 466952
  2163.9 117.1 %collective-permute-start.18 = (f32[8,4864]{1,0:T(8,128)S(1)}, f32[8,4864]{1,0:T(8,128)}, u32[]{:S(2)}, u32[]{:S(2)}) collective-permute-start(f32[8,4864]{1,0:T(8,128)S(1)} %get-tuple-element.417), channel_id=1, source_target_pairs={{0,3},{1,4},{2,5},{3,6},{4,7},{5,8},{6,9},{7,10},{8,11},{9,12},{10... | collective-permute-start | bytes 466952
  2165.8 115.2 %collective-permute-start.17 = (f32[8,4864]{1,0:T(8,128)S(1)}, f32[8,4864]{1,0:T(8,128)}, u32[]{:S(2)}, u32[]{:S(2)}) collective-permute-start(f32[8,4864]{1,0:T(8,128)S(1)} %get-tuple-element.417), channel_id=1, source_target_pairs={{0,2},{1,3},{2,4},{3,5},{4,6},{5,7},{6,8},{7,9},{8,10},{9,11},{10,... | collective-permute-start | bytes 466952
  2170.5 110.5 %collective-permute-start.16 = (f32[8,4864]{1,0:T(8,128)S(1)}, f32[8,4864]{1,0:T(8,128)}, u32[]{:S(2)}, u32[]{:S(2)}) collective-permute-start(f32[8,4864]{1,0:T(8,128)S(1)} %get-tuple-element.417), channel_id=1, source_target_pairs={{0,1},{1,2},{2,3},{3,4},{4,5},{5,6},{6,7},{7,8},{8,9},{9,10},{10,1... | collective-permute-start | bytes 466952
  (120 other events, 6778.7 us)
Sparse Core Ops, SparseCore 0:
  10.4 197.2 all-gather.13
  210.0 192.7 all-gather.15
  405.1 205.5 all-gather.17
  612.8 204.7 all-gather.19
  819.8 204.6 all-gather.21
  1525.3 33.4 reduce-scatter.8
  1561.3 37.8 reduce-scatter.10
  2007.4 229.7 all-reduce.15
where the time goes:
time: 2520 us; the launch traced here: 2500 us
  blocking collectives  1410 us (56%)
  waiting for transfers between devices  448 us (18%)
  local copies, waits for them, and re-layouts  255 us (10%)
  starting transfers between devices  175 us (7%)
  matrix products  129 us (5%)
  other arithmetic  52.3 us (2%)
    unnamed x4, blocking collectives  947 us
    unnamed x164, local copies, waits for them, and re-layouts  210 us
    all_gather x1, waiting for transfers between devices, per_device(): lax.all_gather(w_up.astype(jnp.bfloat16), ('ctx', 'fsdp'), axis=0, tiled=...  193 us
    all_gather x1, waiting for transfers between devices, per_device(): lax.all_gather(w_down.astype(jnp.bfloat16), ('ctx', 'fsdp'), axis=0, tile...  181 us
    all_gather x1, blocking collectives, per_device(): lax.all_gather(w_value.astype(jnp.bfloat16), ('ctx', 'fsdp'), axis=0, til...  181 us
    unnamed x49, starting transfers between devices  174 us
    all_gather x1, blocking collectives, per_device(): lax.all_gather(w_key.astype(jnp.bfloat16), ('ctx', 'fsdp'), axis=0, tiled...  171 us
    all_gather x1, waiting for transfers between devices, per_device(): lax.all_gather(w_gate.astype(jnp.bfloat16), ('ctx', 'fsdp'), axis=0, tile...  73.5 us
  transfers between devices with their start and end apart: 56, of which 3 were waited for; matrix products, arithmetic and copies ran while one was open for 32% of the time, Pallas kernels for 0%

commit v1 on v0

v1 whole, which is shorter than its diff:
```python
import jax
import jax.numpy as jnp
import numpy as np
from jax import lax
from jax.experimental import pallas as pl
from jax.experimental.pallas import tpu as pltpu
from jax.sharding import PartitionSpec as P

HEADS = 14
KV_HEADS = 2
HD = 64
PROMPT = 1024
CONT = 512
PIECE = 64
KBLK = 512
STEP = 10
D = 896
FF = 4864
TOK = 256
DP = 1024
FB = 640
QKV = 1152
ATT = 1152
FFN = 3 * FB
COLS = ATT + FFN
NVEC = 23
LANES = 2 * DP + QKV
LOG_E = 1.4426950408889634
A1 = 640
A2 = 512
HALF = COLS // 2

EPS_NORM = 1e-06
THETA = 1000000.0
CLIP = 1.0
BETA_ONE = 0.9
BETA_TWO = 0.95
ADAM_EPS = 1e-08
STEP_RATES = (0.02, 0.02, 0.02, 0.2, 0.02, 0.02, 0.02, 0.5)
DECAY = 0.1
MASKED = -1e30
MESH = pl.DeviceIdType.MESH
BF = jnp.bfloat16
F32 = jnp.float32
VMEM_LIMIT = 60 * 1024 * 1024


def owner_order():
    order = np.zeros((DP,), np.int32) - 1
    for x in range(4):
        for y in range(4):
            for z in range(4):
                for core in range(2):
                    p = z * 2 + core
                    owner = ((y % 2) * 4 + x) * 16 + z * 4 + (y // 2) * 2 + core
                    block = y * 4 + x if p < 4 else x * 4 + y
                    start = (p // 4) * 512 + block * 32 + (p % 4) * 8
                    order[start : start + 7] = np.arange(7 * owner, 7 * owner + 7)
    return order


def spread_matrix():
    order = owner_order()
    out = np.zeros((D, DP), np.float32)
    for column in range(DP):
        if order[column] >= 0:
            out[order[column], column] = 1.0
    return out

def vector_tables():
    order = owner_order()
    natural = np.concatenate([order, np.where(order < 0, -1, order + D), np.arange(2 * D, 2 * D + QKV)])
    owner_at = np.zeros((128,), np.int32)
    pick = np.zeros((128, DP), np.float32)
    for n in range(128):
        c, f = n // 16, n % 16
        owner_at[n] = ((f // 2 % 2 * 2 + c // 4) * 4 + c % 4) * 8 + f // 4 * 2 + f % 2
        pick[owner_at[n], np.nonzero(order == 7 * n)[0][0] + 7] = 1.0
    holds = np.zeros((128, LANES), np.float32)
    spots = np.zeros((128, LANES), np.float32)
    for lane in range(LANES):
        if natural[lane] >= 0:
            holds[owner_at[natural[lane] // NVEC], lane] = 1.0
            spots[natural[lane] % NVEC, lane] = 1.0
    return pick, spots, holds


def turn_tables():
    frequency = THETA ** (-(np.arange(HD // 2) * (2.0 / HD)))
    out = np.zeros((4, 64, 128), np.float32)
    for n, step in enumerate((PIECE, 1)):
        angles = np.arange(64)[:, None] * float(step) * frequency[None, :]
        out[2 * n] = np.tile(np.cos(angles), (1, 4))
        out[2 * n + 1] = np.tile(np.sin(angles), (1, 4))
    return out


def place():
    c = lax.axis_index("ctx")
    f = lax.axis_index("fsdp")
    return c % 4, (f // 2) % 2 * 2 + c // 4, f // 4, f % 2


def device(x, y, z, core):
    return {"ctx": y % 2 * 4 + x, "fsdp": z * 4 + y // 2 * 2 + core}


def x_peer(me, k):
    x, y, z, core = me
    return device((x + k) % 4, y, z, core)


def y_peer(me, k):
    x, y, z, core = me
    return device(x, (y + k) % 4, z, core)


def z_peer(me, k):
    x, y, z, core = me
    return device(x, y, (z + k) % 4, core)


def pair_peer(me):
    x, y, z, core = me
    return device(x, y // 2 * 2 + 1 - y % 2, z, core)


def other_core(me):
    x, y, z, core = me
    return device(x, y, z, 1 - core)


def line_peer(me, k):
    x, y, z, core = me
    t = (z * 2 + core + k) % 8
    return t, device(x, y, t // 2, t % 2)


def copy(src, dst, send, recv, target):
    return pltpu.make_async_remote_copy(
        src_ref=src, dst_ref=dst, send_sem=send, recv_sem=recv, device_id=target, device_id_type=MESH
    )


def greet(targets):
    barrier = pltpu.get_barrier_semaphore()
    for target in targets:
        pl.semaphore_signal(barrier, inc=1, device_id=target, device_id_type=MESH)
    pl.semaphore_wait(barrier, len(targets))


def line_targets(me):
    return [line_peer(me, k)[1] for k in range(1, 8)]


def ring_targets(me, peer):
    return [peer(me, 1), peer(me, 3)]


class Ring:
    def __init__(self, me, axis, block, half, send, recv):
        self.at = me[axis]
        self.up = (x_peer, y_peer, z_peer)[axis](me, 1)
        self.down = (x_peer, y_peer, z_peer)[axis](me, 3)
        self.half, self.send, self.recv = half, send, recv
        self.close = False

    def one(self, number, arriving=False):
        a = self.at
        ahead, behind, far = (a + 1) % 4, (a + 3) % 4, (a + 2) % 4
        half = (0, 1, 1, 0, 0, 1)[number]
        if arriving:
            t = (behind, behind, ahead, ahead, far, far)[number]
        else:
            t = (a, a, a, a, behind, ahead)[number]
        target = (self.up, self.up, self.down, self.down, self.up, self.down)[number]
        ref = self.half(t, half)
        return copy(ref, ref, self.send.at[number], self.recv.at[number], target)

    def start(self):
        for number in (0, 2, 1, 3):
            self.one(number).start()

    def relay(self):
        self.one(0, True).wait_recv()
        self.one(4).start()
        self.one(2, True).wait_recv()
        self.one(5).start()

    def near(self):
        self.close = True
        self.one(1, True).wait_recv()
        self.one(3, True).wait_recv()

    def finish(self):
        if not self.close:
            self.near()
        self.one(4, True).wait_recv()
        self.one(5, True).wait_recv()

    def drain(self):
        for number in range(6):
            self.one(number).wait_send()


def add_into(ref, other):
    ref[...] = ref[...] + other[...]


class RingSum:
    def __init__(self, me, axis, block, half, tmp, land, land_half, send, recv):
        self.at = me[axis]
        self.up = (x_peer, y_peer, z_peer)[axis](me, 1)
        self.down = (x_peer, y_peer, z_peer)[axis](me, 3)
        self.block, self.half, self.tmp = block, half, tmp
        self.land, self.land_half = land, land_half
        self.send, self.recv = send, recv

    def one(self, number):
        far, ahead, behind = (self.at + 2) % 4, (self.at + 1) % 4, (self.at + 3) % 4
        src, dst, target = (
            (self.half(far, 0), self.tmp(0), self.up), (self.half(far, 1), self.tmp(1), self.down),
            (self.half(ahead, 1), self.land_half(0, 1), self.up),
            (self.half(behind, 0), self.land_half(1, 0), self.down),
            (self.half(ahead, 0), self.land_half(0, 0), self.up),
            (self.half(behind, 1), self.land_half(1, 1), self.down),
        )[number]
        return copy(src, dst, self.send.at[number], self.recv.at[number], target)

    def start_far(self):
        self.one(0).start()
        self.one(1).start()

    def start_near(self):
        self.one(2).start()
        self.one(3).start()

    def start(self):
        self.start_far()
        self.start_near()

    def relay(self):
        ahead, behind = (self.at + 1) % 4, (self.at + 3) % 4
        self.one(0).wait_recv()
        add_into(self.half(ahead, 0), self.tmp(0))
        self.one(4).start()
        self.one(1).wait_recv()
        add_into(self.half(behind, 1), self.tmp(1))
        self.one(5).start()

    def finish(self):
        for number in range(2, 6):
            self.one(number).wait_recv()
        own = self.block(self.at)[...].astype(F32)
        return own + self.land(0)[...].astype(F32) + self.land(1)[...].astype(F32)

    def drain(self):
        for number in range(6):
            self.one(number).wait_send()


class PlaneGather:
    def __init__(self, me, first, second, send, recv):
        x, y, z, core = me

        def rows(ref, a, b, i):
            return ref.at[a, b, pl.ds(16 * i, 16)]

        self.near = [
            Ring(me, 0, lambda t: first.at[y, t], lambda t, i: rows(first, y, t, i), send.at[0], recv.at[0]),
            Ring(me, 1, lambda t: second.at[x, t], lambda t, i: rows(second, x, t, i), send.at[1], recv.at[1]),
        ]
        self.wide = [
            Ring(me, 1, lambda t: first.at[t], lambda t, i: first.at[t, pl.ds(2 * i, 2)], send.at[2], recv.at[2]),
            Ring(me, 0, lambda t: second.at[t], lambda t, i: second.at[t, pl.ds(2 * i, 2)], send.at[3], recv.at[3]),
        ]

    def start(self):
        for ring in self.near:
            ring.start()

    def relay(self):
        for ring in self.near:
            ring.relay()

    def widen(self):
        for one, two in zip(self.near, self.wide):
            one.finish()
            two.start()

    def relay_wide(self):
        for ring in self.wide:
            ring.relay()

    def finish(self):
        for ring in self.wide:
            ring.finish()

    def drain(self):
        for ring in self.near + self.wide:
            ring.drain()


class PlaneSum:
    def __init__(self, me, first, second, tmp_wide, land_wide, tmp, land, send, recv):
        x, y, z, core = me
        self.place = (y, x)
        self.refs = (first, second)

        def wide(axis, ref, n):
            return RingSum(
                me, axis, lambda t: ref.at[t], lambda t, i: ref.at[t, pl.ds(2 * i, 2)],
                lambda i: tmp_wide.at[n, i], lambda i: land_wide.at[n, i],
                lambda i, j: land_wide.at[n, i, pl.ds(2 * j, 2)], send.at[n], recv.at[n],
            )

        def near(axis, ref, a, n):
            return RingSum(
                me, axis, lambda t: ref.at[a, t], lambda t, i: ref.at[a, t, pl.ds(16 * i, 16)],
                lambda i: tmp.at[n, i], lambda i: land.at[n, i],
                lambda i, j: land.at[n, i, pl.ds(16 * j, 16)], send.at[2 + n], recv.at[2 + n],
            )

        self.wide = [wide(1, first, 0), wide(0, second, 1)]
        self.near = [near(0, first, y, 0), near(1, second, x, 1)]

    def start(self):
        for ring in self.wide:
            ring.start()

    def relay_wide(self):
        for ring in self.wide:
            ring.relay()

    def narrow(self):
        for number in range(2):
            total = self.wide[number].finish()
            self.refs[number][self.place[number]] = total.astype(BF)
            self.near[number].start()

    def relay(self):
        for ring in self.near:
            ring.relay()

    def finish(self):
        return [ring.finish() for ring in self.near]

    def drain(self):
        for ring in self.wide + self.near:
            ring.drain()


def plane_sum_scratch(columns):
    return [
        pltpu.VMEM((2, 2, 2, 32, columns), BF), pltpu.VMEM((2, 2, 4, 32, columns), BF),
        pltpu.VMEM((2, 2, 16, columns), BF), pltpu.VMEM((2, 2, 32, columns), BF),
        pltpu.SemaphoreType.DMA((4, 6)), pltpu.SemaphoreType.DMA((4, 6)),
    ]


class LineGather:
    def __init__(self, me, slots, send, recv, csend, crecv):
        self.me, self.slots, self.csend, self.crecv = me, slots, csend, crecv
        x, y, z, core = me
        half = slots.shape[1] // 2
        self.ring = Ring(
            me, 2, lambda t: slots.at[t * 2 + core],
            lambda t, i: slots.at[t * 2 + core, pl.ds(half * i, half)], send, recv,
        )

    def cross(self, k, mine=True):
        x, y, z, core = self.me
        t = (z + k) % 4
        ref = self.slots.at[t * 2 + (core if mine else 1 - core)]
        return copy(ref, ref, self.csend.at[t], self.crecv.at[t], other_core(self.me))

    def start(self):
        self.ring.start()
        self.cross(0).start()

    def relay(self):
        self.ring.relay()
        self.ring.near()
        self.cross(1).start()
        self.cross(3).start()

    def finish_far(self):
        self.ring.finish()
        self.cross(2).start()

    def wait(self, k):
        self.cross(k, False).wait_recv()

    def drain(self):
        self.ring.drain()
        for k in range(4):
            self.cross(k).wait_send()


def line_gather_sems():
    return [dma(6), dma(6), dma(4), dma(4)]


def dma(*n):
    return pltpu.SemaphoreType.DMA(n) if n else pltpu.SemaphoreType.DMA


class Io:
    def __init__(self, ins, outs, in_sem, out_sem):
        self.ins = [pltpu.make_async_copy(far, near, in_sem.at[n]) for n, (far, near) in enumerate(ins)]
        self.outs = [pltpu.make_async_copy(near, far, out_sem.at[n]) for n, (near, far) in enumerate(outs)]
        self.here = 0
        self.left = []

    def start(self, first, last=None):
        for one in self.ins[first:last]:
            one.start()

    def arrive(self, number=None):
        number = len(self.ins) if number is None else number
        while self.here < number:
            self.ins[self.here].wait()
            self.here += 1

    def leave(self, number):
        self.outs[number].start()
        self.left.append(number)

    def close(self):
        self.arrive()
        for number in range(len(self.outs)):
            if number not in self.left:
                self.leave(number)
        for number in self.left:
            self.outs[number].wait()


def comm_call(kernel, out_shape, scratch, number, *args, far_in=(), far_out=(), scalar_in=(), late=None):
    near_in = [n for n in range(len(args)) if n not in far_in and n not in scalar_in]
    near_out = [n for n in range(len(out_shape)) if n not in far_out]

    def body(*refs):
        ins, refs = list(refs[: len(args)]), refs[len(args) :]
        outs, refs = list(refs[: len(out_shape)]), refs[len(out_shape) :]
        near = refs[: len(near_in) + len(near_out)]
        rest, sems = refs[len(near) : -2], refs[-2:]
        io = Io(
            [(ins[n], near[i]) for i, n in enumerate(near_in)],
            [(near[len(near_in) + i], outs[n]) for i, n in enumerate(near_out)],
            *sems,
        )
        io.start(0, late)
        for i, n in enumerate(near_in):
            ins[n] = near[i]
        for i, n in enumerate(near_out):
            outs[n] = near[len(near_in) + i]
        kernel(io, *ins, *outs, *rest)
        io.close()

    spaces = [pltpu.VMEM(args[n].shape, args[n].dtype) for n in near_in]
    spaces += [pltpu.VMEM(out_shape[n].shape, out_shape[n].dtype) for n in near_out]
    if number is None:
        params = pltpu.CompilerParams(vmem_limit_bytes=VMEM_LIMIT)
    else:
        params = pltpu.CompilerParams(
            collective_id=number, has_side_effects=True, vmem_limit_bytes=VMEM_LIMIT
        )
    return pl.pallas_call(
        body,
        out_shape=out_shape,
        in_specs=[pl.BlockSpec(memory_space=pltpu.SMEM if n in scalar_in else pl.ANY) for n in range(len(args))],
        out_specs=tuple(pl.BlockSpec(memory_space=pl.ANY) for _ in out_shape),
        scratch_shapes=[*spaces, *scratch, dma(max(len(near_in), 1)), dma(max(len(near_out), 1))],
        compiler_params=params,
    )(*args)


def shape(*dims, dtype=BF):
    return jax.ShapeDtypeStruct(dims, dtype)


def scale_of(rows):
    return lax.rsqrt(jnp.sum(rows * rows, axis=-1, keepdims=True) * (1.0 / D) + EPS_NORM)


def norm_back(grad, rows, scale, gain):
    weighted = grad * gain
    mean = jnp.sum(weighted * rows, axis=-1, keepdims=True) * (1.0 / D)
    return scale * weighted - rows * (scale * scale * scale * mean), jnp.sum(grad * rows * scale, axis=0)


def dot(left, right):
    return jnp.dot(left, right, preferred_element_type=F32)


def dot_tn(left, right):
    return lax.dot_general(left, right, (((0,), (0,)), ((), ())), preferred_element_type=F32)


def dot_nt(left, right):
    return lax.dot_general(left, right, (((1,), (1,)), ((), ())), preferred_element_type=F32)


def lane(rows):
    return lax.broadcasted_iota(jnp.int32, (rows, 128), 1)


def swap_halves(value):
    low = lane(value.shape[0]) % HD < HD // 2
    return jnp.where(low, pltpu.roll(value, 128 - HD // 2, 1), pltpu.roll(value, HD // 2, 1))


def rope(value, cos, sin):
    return value * cos + swap_halves(value) * sin


def side_of(value, side):
    return jnp.where(lane(value.shape[0]) // HD == side, value, 0.0)


def moved(value, source, target):
    shifted = value if source == target else pltpu.roll(value, HD, 1)
    return side_of(shifted, target)


def local_copy(src, dst, sem):
    return pltpu.make_async_copy(src, dst, sem)


def piece_code(piece):
    later = piece - PROMPT // PIECE
    tail = 4096 * (later // (CONT // PIECE) + 1) + PROMPT + later % (CONT // PIECE) * PIECE
    return jnp.where(later < 0, piece * PIECE, tail)


def forward_kernel(
    io, layout, wq, wk, wv, wvec, wo, spread, wg, wu, wd, tok, cot, turns, pick, spots, holds,
    h_out, n2_out, o_nat, invp, o_low, vec, cos, sin, n1_s, x_s, dy_s, q_ext, keys, values, wa, wb, wdn, wf, dyg, p_far,
    msg, land, msg_b, land_b, w8, pk, s_a, s_b, k_s, v_s, o_ext, p_a, p_b, marks,
    s1s, s1r, s2s, s2r, dns, dnr, fs, fr, as_, ar, bs, br, ls, lr, lcs, lcr, cs, cr, kps, kpr, kxs, kxr, vps, vpr, vxs, vxr, own_sem, p_sem,
):
    me = place()
    x, y, z, core = me
    p = z * 2 + core
    low = y % 2
    greet(line_targets(me) + ring_targets(me, x_peer) + ring_targets(me, y_peer))
    io.arrive(4)

    firsts = []

    def hand_round(out, arrived, send, recv):
        for k in range(1, 8):
            t, target = line_peer(me, k)
            one = copy(out.at[t], arrived.at[p], send.at[k], recv.at[p], target)
            one.start()
            firsts.append(one)
        arrived[p] = out[p]

    def collect(out, arrived, send, recv):
        for k in range(1, 8):
            t, target = line_peer(me, k)
            copy(out.at[t], arrived.at[t], send.at[k], recv.at[t], target).wait_recv()

    def folded(whole, columns):
        return jnp.concatenate([whole[:, :columns], whole[:, columns:]], axis=0).astype(BF)

    def unfolded(arrived, j):
        a = arrived[2 * j].astype(F32)
        b = arrived[2 * j + 1].astype(F32)
        return jnp.concatenate([jnp.concatenate([a[:8], b[:8]], 0), jnp.concatenate([a[8:], b[8:]], 0)], 1).astype(BF)

    def blank(columns):
        return jnp.zeros((8, columns), F32)

    w8[...] = jnp.zeros_like(w8)
    first = 0
    for ref in (wq, wk, wv):
        w8[0:7, first : first + ref.shape[1]] = ref[...]
        first += ref.shape[1]
    w8[7:8, 0:NVEC] = wvec[...]
    halves = (
        folded(jnp.concatenate([w8[:, 0:A1], blank(128)], 1), 384),
        folded(jnp.concatenate([w8[:, A1:QKV], blank(256)], 1), 384),
    )
    for t in range(8):
        msg[t] = halves[t % 2]
    hand_round(msg, land, s1s, s1r)
    io.arrive(9)
    w8[0:7, QKV : QKV + DP] = dot(wo[...].astype(BF), spread[...])
    for n, ref in enumerate((wg, wu, wd)):
        w8[0:7, QKV + DP + FF * n : QKV + DP + FF * (n + 1)] = ref[...]
    for t in range(8):
        base = QKV + DP + FB * t if t < 6 else QKV + DP + FB * 6 + 512 * (t - 6)
        width = FB if t < 6 else 512
        at = QKV + A2 * (t % 2)
        pieces = [w8[:, at : at + A2]]
        for n in range(3):
            pieces.append(w8[:, base + FF * n : base + FF * n + width])
            if width < FB:
                pieces.append(blank(FB - width))
        pieces.append(blank(128))
        msg_b[t] = folded(jnp.concatenate(pieces, axis=1), 1280)
    hand_round(msg_b, land_b, s2s, s2r)
    io.arrive()
    x_s[...] = dot(tok[...], spread[...])
    io.leave(9)
    dy_s[...] = dot(cot[...], spread[...]).astype(BF)
    io.leave(10)
    own_dy = local_copy(dy_s, dyg.at[p], own_sem.at[2])
    own_dy.start()
    collect(msg, land, s1s, s1r)
    for j in range(4):
        rows = slice(16 * (j % 2), 16 * (j % 2) + 16)
        at = (y, x) if j < 2 else (x, y)
        wa[core, j // 2, at[0], at[1], rows, :] = unfolded(land, j)[:, 0:A1]
    att = PlaneGather(me, wa.at[core, 0], wa.at[core, 1], as_, ar)
    out = PlaneGather(me, wb.at[core, 0], wb.at[core, 1], bs, br)
    ffn = PlaneGather(me, wf.at[0], wf.at[1], fs, fr)
    down = [
        Ring(me, n, lambda t, n=n: None, lambda t, i, n=n: wdn.at[n, t, pl.ds(16 * i, 16)], dns.at[n], dnr.at[n])
        for n in range(2)
    ]
    line = LineGather(me, dyg, ls, lr, lcs, lcr)
    att.start()
    codes = jnp.zeros((1, 128), jnp.int32)
    for t in range(32):
        block = t // 4
        code = piece_code(layout[0, (block % 2 * 4 + block // 2) * 4 + t % 4])
        codes = jnp.where(lane(1) % HD == t, code, codes)
    sign = jnp.where(lane(PIECE) % HD < HD // 2, -1.0, 1.0)
    for i in range(4):
        code = piece_code(layout[0, 4 * (low * 4 + x) + i])
        rows = slice(PIECE * i, PIECE * i + PIECE)
        seen = (codes <= code) & ((codes < PROMPT) | (codes >= code // 4096 * 4096))
        barred = jnp.where((lane(1) % HD < 32) & jnp.logical_not(seen), MASKED, 0.0)
        marks[rows, :] = jnp.zeros((PIECE, 128), F32) + barred
        number = code % 4096 // PIECE
        cos_far, sin_far = turns[0, pl.ds(number, 1), :], turns[1, pl.ds(number, 1), :]
        cos_near, sin_near = turns[2, 0:PIECE, :], turns[3, 0:PIECE, :]
        cos[rows, :] = cos_far * cos_near - sin_far * sin_near
        sin[rows, :] = (sin_far * cos_near + cos_far * sin_near) * sign
    io.leave(6)
    io.leave(7)
    att.relay()
    own_dy.wait()
    line.start()
    att.widen()
    collect(msg_b, land_b, s2s, s2r)
    for j in range(4):
        rows = slice(16 * (j % 2), 16 * (j % 2) + 16)
        at = (y, x) if j < 2 else (x, y)
        block = unfolded(land_b, j)
        wb[core, j // 2, at[0], at[1], rows, :] = block[:, 0:A2]
        pk[j // 2, rows, :] = block[:, A2 : A2 + 2 * FB]
        wdn[j // 2, (x, y)[j // 2], rows, :] = block[:, A2 + 2 * FB : A2 + FFN]
    out.start()
    owns = [
        local_copy(pk.at[0], wf.at[0, y, x], own_sem.at[0]), local_copy(pk.at[1], wf.at[1, x, y], own_sem.at[1])
    ]
    for one in owns:
        one.start()
    att.relay_wide()
    out.relay()
    for one in owns:
        one.wait()
    ffn.start()
    att.finish()
    cross = [
        copy(ref.at[core], ref.at[core], cs.at[n], cr.at[n], other_core(me)) for n, ref in enumerate((wa, wb))
    ]
    crossed = [
        copy(ref.at[1 - core], ref.at[1 - core], cs.at[n], cr.at[n], other_core(me)) for n, ref in enumerate((wa, wb))
    ]
    cross[0].start()
    out.widen()
    crossed[0].wait_recv()

    table = dot(pick[...], wide(wa, 0, 0, 128)).astype(BF)
    vec[...] = jnp.sum(dot(table, spots[...]) * holds[...].astype(F32), axis=0, keepdims=True)
    xs = x_s[...]
    n1_s[...] = (xs * scale_of(xs) * vec[:, 0:DP]).astype(BF)
    second = dot(n1_s[...], wide(wa, 1, 0, QKV - A1)) + vec[:, 2 * DP + A1 :]
    kv_pre = second[:, D - A1 :]
    keys[x, low] = rope(kv_pre[:, 0:128], cos[...], sin[...]).astype(BF)
    values[x, low] = kv_pre[:, 128:256].astype(BF)
    key_pair = copy(keys.at[x, low], keys.at[x, low], kps, kpr, pair_peer(me))
    key_pair.start()
    key_ring = Ring(me, 0, lambda t: keys.at[t], lambda t, i: keys.at[t, i], kxs, kxr)
    value_ring = Ring(
        me, 0, lambda t: values.at[t, low], lambda t, i: values.at[t, low, pl.ds(128 * i, 128)], vxs, vxr
    )
    value_ring.start()
    value_pair = copy(values.at[:, low], values.at[:, low], vps, vpr, pair_peer(me))
    io.leave(5)
    io.leave(8)
    io.leave(14)
    q_pre = jnp.concatenate(
        [dot(n1_s[...], wide(wa, 0, 0, A1)) + vec[:, 2 * DP : 2 * DP + A1], second[:, : D - A1]], axis=1
    )
    copy(keys.at[x, 1 - low], keys.at[x, 1 - low], kps, kpr, pair_peer(me)).wait_recv()
    key_ring.start()
    value_ring.relay()
    for head in range(HEADS):
        block = q_pre[:, 128 * (head // 2) : 128 * (head // 2) + 128]
        turned = rope(block, cos[...], sin[...]) * (HD**-0.5 * LOG_E)
        turned = moved(turned, head % 2, head // 7)
        q_ext[head] = (turned + side_of(marks[...], 1 - head // 7)).astype(BF)
    io.leave(11)
    value_ring.finish()
    value_pair.start()
    key_ring.relay()
    out.relay_wide()
    ffn.relay()
    ffn.widen()
    line.relay()
    key_ring.finish()
    io.leave(12)
    out.finish()
    cross[1].start()
    for ring in down:
        ring.start()
    all_keys = keys[...].reshape(8 * TOK, 128).astype(F32)
    piece = lax.broadcasted_iota(jnp.int32, (8 * TOK, 128), 0) // PIECE
    marked = jnp.where(lane(8 * TOK) % HD == piece, 1.0, 0.0)
    for j in range(2):
        k_s[j] = jnp.where(lane(8 * TOK) // HD == j, all_keys, marked).astype(BF)
    apart = lax.broadcasted_iota(jnp.int32, (TOK, TOK), 1) - lax.broadcasted_iota(jnp.int32, (TOK, TOK), 0)
    same = lax.broadcasted_iota(jnp.int32, (TOK, TOK), 1) // PIECE == lax.broadcasted_iota(jnp.int32, (TOK, TOK), 0) // PIECE
    diagonal = pl.ds(pl.multiple_of((x * 2 + low) * TOK, TOK), TOK)
    copy(values.at[:, 1 - low], values.at[:, 1 - low], vps, vpr, pair_peer(me)).wait_recv()
    io.leave(13)
    v_s[:, 0:128] = values[...].reshape(8 * TOK, 128)
    v_s[:, 128:256] = jnp.ones((8 * TOK, 128), BF)
    invp[...] = jnp.zeros_like(invp)

    p_s = (p_a, p_b)
    s_s = (s_a, s_b)

    def put(i, j):
        return local_copy(p_s[j].at[i % 2], p_far.at[7 * j + i], p_sem.at[j, i % 2])

    def attend(i, carry):
        @pl.when(i >= 2)
        def _():
            for j in range(2):
                put(i, j).wait()

        for j in range(2):
            s_s[j][...] = dot_nt(q_ext[7 * j + i], k_s[j])
        inverse_all = invp[...]
        for j in range(2):
            s_s[j][:, diagonal] = jnp.where(same & (apart > 0), MASKED, s_s[j][:, diagonal])
            scores = s_s[j][...]
            numerators = jnp.exp2(scores - jnp.max(scores, axis=1, keepdims=True)).astype(BF)
            p_s[j][i % 2] = numerators
            both = dot(numerators, v_s[...])
            inverse = 1.0 / both[:, 128:256]
            o_ext[7 * j + i] = side_of(both[:, 0:128] * inverse, j)
            inverse_all = jnp.where(lane(TOK) == 7 * j + i, inverse, inverse_all)
        invp[...] = inverse_all
        for j in range(2):
            put(i, j).start()
        return carry

    lax.fori_loop(0, 4, attend, 0)
    crossed[1].wait_recv()
    io.leave(15)
    ffn.relay_wide()
    for ring in down:
        ring.relay()
    line.finish_far()
    lax.fori_loop(4, 7, attend, 0)
    for block in range(7):
        pieces = [moved(o_ext[2 * block + e], (2 * block + e) // 7, e) for e in range(2)]
        o_nat[:, 128 * block : 128 * block + 128] = pieces[0] + pieces[1]

    o_low[...] = dot(o_nat[...].astype(BF), spread[...]).astype(BF)
    for n in range(2):
        cols = slice(A2 * n, A2 * n + A2)
        h_out[:, cols] = x_s[:, cols] + dot(o_low[...], wide(wb, n, 0, A2))
    h = h_out[...]
    n2_out[...] = (h * scale_of(h) * vec[:, DP : 2 * DP]).astype(BF)
    for number in range(5):
        io.leave(number)
    for ring in down:
        ring.finish()
    io.leave(16)
    ffn.finish()
    for k in range(4):
        line.wait(k)
    for i in (5, 6):
        for j in range(2):
            put(i, j).wait()
    line.drain()
    att.drain()
    out.drain()
    ffn.drain()
    for ring in down:
        ring.drain()
    key_ring.drain()
    value_ring.drain()
    key_pair.wait_send()
    value_pair.wait_send()
    for one in firsts + cross:
        one.wait_send()


def wide(ref, side, first, columns):
    return ref[side, :, :, :, :, first : first + columns].reshape(DP, columns)


def forward(*args):
    row = pltpu.VMEM
    return comm_call(
        forward_kernel,
        (
            shape(TOK, DP, dtype=F32), shape(TOK, DP), shape(TOK, D, dtype=F32), shape(TOK, 128, dtype=F32),
            shape(TOK, DP), shape(1, LANES, dtype=F32), shape(TOK, 128, dtype=F32), shape(TOK, 128, dtype=F32),
            shape(TOK, DP), shape(TOK, DP, dtype=F32), shape(TOK, DP), shape(HEADS, TOK, 128),
            shape(4, 2, TOK, 128), shape(4, 2, TOK, 128),
            shape(2, 2, 4, 4, 32, A1), shape(2, 2, 4, 4, 32, A2), shape(2, 4, 32, FB), shape(2, 4, 4, 32, 2 * FB),
            shape(8, TOK, DP), shape(HEADS, TOK, 8 * TOK),
        ),
        [
            row((8, 16, 384), BF), row((8, 16, 384), BF), row((8, 16, 1280), BF), row((8, 16, 1280), BF),
            row((8, QKV + DP + 3 * FF), F32), row((2, 32, 2 * FB), BF), row((TOK, 8 * TOK), F32),
            row((TOK, 8 * TOK), F32), row((2, 8 * TOK, 128), BF), row((8 * TOK, 256), BF),
            row((HEADS, TOK, 128), F32), row((2, TOK, 8 * TOK), BF), row((2, TOK, 8 * TOK), BF),
            row((TOK, 128), F32),
            dma(8), dma(8), dma(8), dma(8), dma(2, 6), dma(2, 6), dma(4, 6), dma(4, 6), dma(4, 6), dma(4, 6), dma(4, 6), dma(4, 6),
            *line_gather_sems(), dma(2), dma(2), dma(), dma(), dma(6), dma(6), dma(), dma(), dma(6), dma(6),
            dma(3), dma(2, 2),
        ],
        1, *args, far_out=(17, 18, 19), scalar_in=(0,),
    )


def ffn_kernel(
    io, n2, wf, dyg, wdn, dn2_out, reduced, y_far, g_far,
    wd, grads, grads_d, n2g, dparts, yparts, got, tmp, land, hid_all, dgu_all, dhid_all, gu_s,
    f_tw, f_lw, f_t, f_l, f_s, f_r, leave, wds, wdr, ls, lr, lcs, lcr, gs, gr, ds, dr,
):
    me = place()
    x, y, z, core = me
    rows = [
        pltpu.make_async_copy(wdn.at[0], wd.at[0, y], leave.at[0]),
        pltpu.make_async_copy(wdn.at[1], wd.at[1, x], leave.at[1]),
    ]
    for one in rows:
        one.start()
    greet(ring_targets(me, z_peer) + [other_core(me)] + ring_targets(me, x_peer) + ring_targets(me, y_peer))
    io.arrive(1)
    n2g[z * 2 + core] = n2[...]
    line = LineGather(me, n2g, ls, lr, lcs, lcr)
    line.start()
    for one in rows:
        one.wait()
    gathers = [
        Ring(
            me, 1 - n, lambda t: None, lambda t, i, n=n: wd.at[n, t, pl.ds(2 * i, 2)], wds.at[n], wdr.at[n]
        )
        for n in range(2)
    ]
    for ring in gathers:
        ring.start()

    def both():
        return wf[...].reshape(DP, 2 * FB)

    def down():
        return wd[...].reshape(DP, FB)

    def slot(k, side):
        return (z + k) % 4 * 2 + side

    def one(s, gu=None):
        gu = dot(n2g[s], both()) if gu is None else gu
        gate, up = gu[:, :FB], gu[:, FB:]
        sig = 1.0 / (1.0 + jnp.exp(-gate))
        act = gate * sig
        hid_all[s] = (act * up).astype(BF)
        dhid = dhid_all[s]
        dgu_all[s, :, :FB] = (dhid * up * (sig + act * (1.0 - sig))).astype(BF)
        dgu_all[s, :, FB:] = (dhid * act).astype(BF)
        dparts[s] = dot_nt(dgu_all[s], both()).astype(BF)

    def pair(n, ref, k):
        t = (z + k) % 4
        return copy(ref.at[t * 2 + 1 - core], got.at[n, t], gs.at[n, t], gr.at[n, t], other_core(me))

    def join(n, ref, k):
        t = (z + k) % 4
        pair(n, ref, k).wait_recv()
        add_into(ref.at[t * 2 + core], got.at[n, t])

    def compute(k, between=None):
        if between is None:

            def body(i, carry):
                side = (1 - core) * (1 - i) + core * i
                one(slot(k, side), gu_s[side] if k == 0 else None)
                return carry

            lax.fori_loop(0, 2, body, 0)
        else:
            lax.fori_loop(0, 1, lambda i, carry: (one(slot(k, 1 - core)), carry)[1], 0)
            between()
            lax.fori_loop(0, 1, lambda i, carry: (one(slot(k, core)), carry)[1], 0)
        pair(0, dparts, k).start()

    dsum = RingSum(
        me, 2, lambda t: dparts.at[t * 2 + core], lambda t, i: dparts.at[t * 2 + core, pl.ds(128 * i, 128)],
        lambda i: tmp.at[i], lambda i: land.at[i], lambda i, j: land.at[i, pl.ds(128 * j, 128)], ds, dr,
    )

    def after_first():
        join(0, dparts, 1)
        dsum.one(2).start()

    def after_far():
        join(0, dparts, 2)
        dsum.start_far()

    def hidden_grads(first, last):
        def body(i, carry):
            s = (z * 2 + i) % 8
            dhid_all[s] = dot(dyg[s], down())
            return carry

        lax.fori_loop(first, last, body, 0)

    def own_gates(side, carry):
        gu_s[side] = dot(n2g[z * 2 + side], both())
        return carry

    io.arrive()
    line.wait(0)
    lax.fori_loop(0, 2, own_gates, 0)
    for ring in gathers:
        ring.relay()
    for ring in gathers:
        ring.finish()
    hidden_grads(0, 2)
    compute(0)
    hidden_grads(2, 8)
    line.relay()
    line.wait(1)
    line.wait(3)
    compute(1)
    join(0, dparts, 0)
    line.finish_far()
    line.wait(2)
    compute(2, after_first)
    compute(3, after_far)

    fsum = PlaneSum(me, grads.at[0], grads.at[1], f_tw, f_lw, f_t, f_l, f_s, f_r)
    leaves = []

    def weight_grads(left, right, into, width, first, last):
        for m in range(first, last):
            rows = left[:, :, 256 * m : 256 * m + 256].reshape(8 * TOK, 256)
            value = dot_tn(rows, right[...].reshape(8 * TOK, width)).astype(BF)
            into[m // 2, 2 * (m % 2) : 2 * (m % 2) + 2] = value.reshape(2, 4, 32, width)

    def outputs(k, carry):
        for side in range(2):
            yparts[slot(k, side)] = dot_nt(hid_all[slot(k, side)], down()).astype(BF)
        return carry

    weight_grads(n2g, dgu_all, grads, 2 * FB, 0, 1)
    join(0, dparts, 3)
    dsum.one(3).start()
    weight_grads(n2g, dgu_all, grads, 2 * FB, 1, 2)
    fsum.wide[0].start()
    weight_grads(n2g, dgu_all, grads, 2 * FB, 2, 4)
    fsum.wide[1].start()
    dsum.relay()
    weight_grads(dyg, hid_all, grads_d, FB, 0, 4)
    leaves.append(pltpu.make_async_copy(grads_d, g_far, leave.at[4]))
    leaves[0].start()
    fsum.wide[0].relay()
    lax.fori_loop(0, 2, outputs, 0)
    for k in range(2):
        pair(1, yparts, k).start()
    fsum.wide[1].relay()
    dn2_out[...] = dsum.finish()
    io.leave(0)
    lax.fori_loop(2, 4, outputs, 0)
    for k in range(2, 4):
        pair(1, yparts, k).start()
    for k in range(4):
        join(1, yparts, k)
        t = (z + k) % 4
        one_out = pltpu.make_async_copy(yparts.at[t * 2 + core], y_far.at[t], leave.at[k])
        one_out.start()
        leaves.append(one_out)
    for n in range(2):
        reduced[n] = fsum.wide[n].finish().astype(BF)
    io.leave(1)
    for ring in fsum.wide + gathers:
        ring.drain()
    line.drain()
    for n, ref in enumerate((dparts, yparts)):
        for k in range(4):
            pair(n, ref, k).wait_send()
    dsum.drain()
    for one_out in leaves:
        one_out.wait()


def feed_forward(n2, wf, dyg, wdn):
    slots = pltpu.VMEM((8, TOK, DP), BF)
    return comm_call(
        ffn_kernel,
        (shape(TOK, DP, dtype=F32), shape(2, 4, 32, 2 * FB), shape(4, TOK, DP), shape(2, 4, 4, 32, FB)),
        [
            pltpu.VMEM((2, 4, 4, 32, FB), BF), pltpu.VMEM((2, 4, 4, 32, 2 * FB), BF), pltpu.VMEM((2, 4, 4, 32, FB), BF),
            slots, slots, slots, pltpu.VMEM((2, 4, TOK, DP), BF),
            pltpu.VMEM((2, TOK // 2, DP), BF), pltpu.VMEM((2, TOK, DP), BF),
            pltpu.VMEM((8, TOK, FB), BF), pltpu.VMEM((8, TOK, 2 * FB), BF), pltpu.VMEM((8, TOK, FB), F32),
            pltpu.VMEM((2, TOK, 2 * FB), F32),
            *plane_sum_scratch(2 * FB), dma(6), dma(2, 6), dma(2, 6),
            *line_gather_sems(), dma(2, 4), dma(2, 4), dma(6), dma(6),
        ],
        2, n2, wf, dyg, wdn, far_in=(3,), far_out=(2, 3),
    )


def plane_peer(me, k):
    x, y, z, core = me
    t = (y * 4 + x + k) % 16
    return t, device(t % 4, t // 4, z, core)


def fold_squares(value):
    total = jnp.zeros((8, 128), F32)
    for b in range(value.shape[1] // 128):
        piece = value[:, 128 * b : 128 * b + 128]
        total = total + piece * piece
    return total


def backward_kernel(
    io, reduced, own, yb, dn2, h, dy, vec, o_low, wb, spread, invp, o_nat, q_ext, k_s, v_in,
    n1, xs, wa, cos, sin, spots, holds, p_far,
    result, input_grad, grads, att_grads, norm,
    ytmp, yland, ag0, ag1, got0, got1, bland, ent, eland, asums, aland, sums, squares, lsq, psq,
    v_s, do_s, do_ext, do_t, q_t, dq_ext, dkt, dvt, p_s, ds_s, kvp, kvtmp, kvland, give, take, dh, dqkv, dn1,
    n_t, n_l, n_s, n_r, f_tw, f_lw, f_t, f_l, f_s, f_r, a_tw, a_lw, a_t, a_l, a_s, a_r,
    p_sem, bs, br, es, er, ys, yr, cs, cr, ks, kr, kps, kpr, lfs, lfr, las, lar, qs, qr, ts, tr,
):
    me = place()
    x, y, z, core = me
    p = z * 2 + core
    q = y * 4 + x
    low = y % 2

    units = [(0, 2), (2, 2), (4, 2), (6, 1), (7, 2), (9, 2), (11, 2), (13, 1)]

    def get(unit):
        head, count = units[unit]
        rows = pl.ds(0, count)
        return local_copy(p_far.at[pl.ds(head, count)], p_s.at[unit % 2, rows], p_sem.at[unit % 2])

    for unit in range(2):
        get(unit).start()
    io.start(15)
    greet(line_targets(me) + [plane_peer(me, k)[1] for k in range(1, 16)])
    io.arrive(3)
    fsum = PlaneSum(me, own.at[0], own.at[1], f_tw, f_lw, f_t, f_l, f_s, f_r)
    asum = PlaneSum(me, got0.at[0], got0.at[1], a_tw, a_lw, a_t, a_l, a_s, a_r)

    def send_narrow():
        for k in range(1, 16):
            t, target = plane_peer(me, k)
            copy(got1.at[t], bland.at[q], bs.at[k], br.at[q], target).start()
        bland[q] = got1[q]

    def by_place(value):
        for t in range(16):
            turned = t % 4 * 4 + t // 4
            yield t, value[32 * t : 32 * t + 32], value[512 + 32 * turned : 544 + 32 * turned]

    ysum = RingSum(
        me, 2, lambda t: yb.at[t], lambda t, i: yb.at[t, pl.ds(128 * i, 128)],
        lambda i: ytmp.at[i], lambda i: yland.at[i], lambda i, j: yland.at[i, pl.ds(128 * j, 128)], ys, yr,
    )
    nears = [
        RingSum(
            me, n, lambda t, n=n: reduced.at[n, t], lambda t, i, n=n: reduced.at[n, t, pl.ds(16 * i, 16)],
            lambda i, n=n: n_t.at[n, i], lambda i, n=n: n_l.at[n, i],
            lambda i, j, n=n: n_l.at[n, i, pl.ds(16 * j, 16)], n_s.at[n], n_r.at[n],
        )
        for n in range(2)
    ]
    for ring in nears:
        ring.start()
    fsum.start()
    ysum.start()

    io.arrive(10)
    scale_two = scale_of(h[...])
    dh_part, dgain_two = norm_back(dn2[...], h[...], scale_two, vec[:, DP : 2 * DP])
    dh[...] = dy[...].astype(F32) + dh_part
    da = dh[...].astype(BF)
    dwo = dot_tn(o_low[...], da).astype(BF)
    ag0[...] = dwo[:, 0:D].reshape(2, 4, 4, 32, D)
    ag1[...] = jnp.zeros_like(ag1)
    for t, one, two in by_place(dwo[:, D:DP]):
        ag1[t, 0:32, 0:128] = one
        ag1[t, 32:64, 0:128] = two

    def give_part(n, number):
        return copy((ag0, ag1)[n], (got0, got1)[n], cs.at[number, n], cr.at[number, n], other_core(me))

    @pl.when(core == 0)
    def _():
        give_part(0, 0).start()
        give_part(1, 0).start()

    do_far = (dot_nt(da[:, 0:A2], wide(wb, 0, 0, A2)) + dot_nt(da[:, A2:DP], wide(wb, 1, 0, A2))).astype(BF)
    do_s[...] = dot_nt(do_far, spread[...]).astype(BF)
    io.arrive(15)
    all_values = v_in[...].reshape(8 * TOK, 128).astype(F32)
    for j in range(2):
        ones = jnp.where(lane(8 * TOK) % HD < 3, 1.0, 0.0)
        v_s[j] = jnp.where(lane(8 * TOK) // HD == j, all_values, ones).astype(BF)

    def prepare(unit):
        first, count = units[unit]
        for spot in range(count):
            head = first + spot
            j = head // 7
            lanes = slice(128 * (head // 2), 128 * (head // 2) + 128)
            inverse = invp[:, head : head + 1]
            block = side_of(do_s[:, lanes].astype(F32), head % 2)
            rest = -jnp.sum(block * o_nat[:, lanes], axis=1, keepdims=True) * inverse
            value = moved(block * inverse, head % 2, j)
            for n in range(3):
                part = rest.astype(BF).astype(F32)
                value = jnp.where(lane(TOK) == HD * (1 - j) + n, part, value)
                rest = rest - part
            do_ext[head] = value.astype(BF)
            columns = slice(TOK * spot, TOK * spot + TOK)
            do_t[unit, :, columns] = value.T[HD * j : HD * j + HD].astype(BF)
            q_t[unit, :, columns] = q_ext[head].astype(F32).T[HD * j : HD * j + HD].astype(BF)

    for ring in nears:
        ring.relay()
    prepare(0)
    dkt[...] = jnp.zeros_like(dkt)
    dvt[...] = jnp.zeros_like(dvt)

    @pl.when(core == 1)
    def _():
        give_part(0, 0).wait_recv()
        add_into(got0, ag0)
        asum.start()
        give_part(1, 0).wait_recv()
        add_into(got1, ag1)
        send_narrow()

    def heads(unit):
        head, count = units[unit]
        j = head // 7
        half = slice(HD * j, HD * j + HD)
        rows = count * TOK
        base = 2 * TOK if unit == 7 else 0
        get(unit).wait()
        dp = dot_nt(do_ext[head : head + count].reshape(rows, 128), v_s[j])
        numerators = p_s[unit % 2, 0:count].reshape(rows, 8 * TOK)
        dvt[half, :] += dot(do_t[unit, :, 0:rows], numerators)
        ds_s[base : base + rows, :] = dp.astype(BF) * numerators
        if unit + 1 < len(units):
            prepare(unit + 1)
        dkt[half, :] += dot(q_t[unit, :, 0:rows], ds_s[base : base + rows, :])
        if unit < 6:
            query_grads(head, count)
        if unit + 2 < len(units):
            get(unit + 2).start()

    def query_grads(head, count):
        value = dot(ds_s[0 : count * TOK, :], k_s[...].reshape(8 * TOK, 128))
        dq_ext[head : head + count] = value.reshape(count, TOK, 128)

    def kv_sum(j):
        return RingSum(
            me, 0, lambda t: kvp.at[j, t], lambda t, i: kvp.at[j, t, i],
            lambda i: kvtmp.at[j, i], lambda i: kvland.at[j, i], lambda i, n: kvland.at[j, i, n],
            ks.at[j], kr.at[j],
        )

    def kv_pack(j):
        for t in range(8):
            lanes = slice(256 * t, 256 * t + 256)
            kvp[j, t // 2, t % 2, 0:HD, :] = (dkt[HD * j : HD * j + HD, lanes] * (1.0 / LOG_E)).astype(BF)
            kvp[j, t // 2, t % 2, HD:128, :] = dvt[HD * j : HD * j + HD, lanes].astype(BF)

    def kv_pair(j):
        return copy(give.at[j, 1 - low], take.at[j], kps.at[j], kpr.at[j], pair_peer(me))

    def kv_cross(j):
        give[j] = kv_sums[j].finish().astype(BF)
        kv_pair(j).start()

    def kv_total(j):
        kv_pair(j).wait_recv()
        return give[j, low].astype(F32) + take[j].astype(F32)

    kv_sums = [kv_sum(0), kv_sum(1)]
    heads(0)
    heads(1)
    fsum.relay_wide()
    ysum.relay()

    @pl.when(core == 1)
    def _():
        asum.relay_wide()

    heads(2)
    heads(3)
    kv_pack(0)
    kv_sums[0].start()
    fsum.narrow()

    @pl.when(core == 1)
    def _():
        asum.narrow()

    heads(4)
    heads(5)
    kv_sums[0].relay()
    fsum.relay()

    @pl.when(core == 1)
    def _():
        asum.relay()

    heads(6)
    kv_cross(0)
    heads(7)
    kv_pack(1)
    kv_sums[1].start()

    query_grads(11, 3)
    io.arrive()
    for block in range(7):
        pieces = [moved(dq_ext[2 * block + e], (2 * block + e) // 7, e) for e in range(2)]
        turned = rope((pieces[0] + pieces[1]) * HD**-0.5, cos[...], -sin[...])
        dqkv[:, 128 * block : 128 * block + 128] = turned.astype(BF)
    @pl.when(core == 0)
    def _():
        give_part(0, 0).wait_send()
        give_part(1, 0).wait_send()

    ag0[...] = dot_tn(n1[...], dqkv[:, 0:D]).astype(BF).reshape(2, 4, 4, 32, D)

    @pl.when(core == 1)
    def _():
        give_part(0, 1).start()

    kv_sums[1].relay()
    dn1[...] = dot_nt(dqkv[:, 0:A1], wide(wa, 0, 0, A1)) + dot_nt(dqkv[:, A1:D], wide(wa, 1, 0, D - A1))
    kv_cross(1)

    @pl.when(core == 0)
    def _():
        give_part(0, 1).wait_recv()
        add_into(got0, ag0)
        asum.start()

    dkv = [kv_total(0), kv_total(1)]
    dk = jnp.concatenate([dkv[0][0:HD], dkv[1][0:HD]], axis=0).T
    dv = jnp.concatenate([dkv[0][HD:128], dkv[1][HD:128]], axis=0).T
    dqkv[:, D : D + 128] = rope(dk, cos[...], -sin[...]).astype(BF)
    dqkv[:, D + 128 : QKV] = dv.astype(BF)
    for t, one, two in by_place(dot_tn(n1[...], dqkv[:, D:QKV]).astype(BF)):
        ag1[t, 0:32] = one
        ag1[t, 32:64] = two

    @pl.when(core == 1)
    def _():
        give_part(1, 1).start()

    @pl.when(core == 0)
    def _():
        asum.relay_wide()
        give_part(1, 1).wait_recv()
        add_into(got1, ag1)
        send_narrow()

    dn1_all = dn1[...] + dot_nt(dqkv[:, D:QKV], wide(wa, 1, D - A1, QKV - D))
    scale_one = scale_of(xs[...])
    dx_part, dgain_one = norm_back(dn1_all, xs[...], scale_one, vec[:, 0:DP])
    dbias = jnp.sum(dqkv[...].astype(F32), axis=0, keepdims=True)
    dvec = jnp.concatenate([dgain_one[None], dgain_two[None], dbias], axis=1)
    dvec_high = dvec.astype(BF).astype(F32)
    entries = jnp.zeros((128, 128), F32)
    for part in (dvec_high, dvec - dvec_high):
        entries = entries + dot_nt((holds[...].astype(F32) * part).astype(BF), spots[...])
    ent[...] = entries.reshape(16, 8, 128)
    sent = []
    for k in range(1, 16):
        t, target = plane_peer(me, k)
        one = copy(ent.at[t], eland.at[q], es.at[k], er.at[q], target)
        one.start()
        sent.append(one)
    eland[q] = ent[q]

    @pl.when(core == 0)
    def _():
        asum.narrow()

    sum_f = fsum.finish()
    for i in range(2):
        sums[4 * i : 4 * i + 4, :, 0 : 2 * FB] = nears[i].finish().reshape(4, 8, 2 * FB)
        sums[4 * i : 4 * i + 4, :, 2 * FB : FFN] = sum_f[i].reshape(4, 8, FB)
    for k in range(1, 8):
        t, target = line_peer(me, k)
        one = copy(sums.at[t], grads.at[p], lfs.at[k], lfr.at[p], target)
        one.start()
        sent.append(one)

    @pl.when(core == 0)
    def _():
        asum.relay()

    sum_a = asum.finish()
    sum_b = jnp.zeros((64, 256), F32)
    entry = jnp.zeros((8, 128), F32)
    for k in range(1, 16):
        t, target = plane_peer(me, k)
        copy(got1.at[t], bland.at[t], bs.at[k], br.at[t], target).wait_recv()
        copy(ent.at[t], eland.at[t], es.at[k], er.at[t], target).wait_recv()
    for t in range(16):
        sum_b = sum_b + bland[t].astype(F32)
        entry = entry + eland[t]
    last = lax.broadcasted_iota(jnp.int32, (4, 8, 128), 1) == 7
    for i in range(2):
        added = jnp.where(last, entry[4 * i : 4 * i + 4].reshape(4, 1, 128), 0.0)
        narrow = sum_b[32 * i : 32 * i + 32].reshape(4, 8, 256)
        wide_rows = jnp.concatenate(
            [sum_a[i].reshape(4, 8, D), narrow[:, :, 0:128] + added, narrow[:, :, 128:256], jnp.zeros((4, 8, 128), F32)],
            axis=2,
        )
        asums[4 * i : 4 * i + 4] = jnp.concatenate(
            [wide_rows[:, :, 0:640], wide_rows[:, :, 640:1280]], axis=1
        ).astype(BF)
    for k in range(1, 8):
        t, target = line_peer(me, k)
        one = copy(asums.at[t], aland.at[p], las.at[k], lar.at[p], target)
        one.start()
        sent.append(one)
    aland[p] = asums[p]
    grads[p] = sums[p]
    result[...] = dot_nt((h[...] + ysum.finish()).astype(BF), spread[...]).astype(BF)
    io.leave(0)
    rest = dh[...] + dx_part
    total = jnp.zeros((TOK, D), F32)
    for _ in range(3):
        part = rest.astype(BF)
        total = total + dot_nt(part, spread[...])
        rest = rest - part.astype(F32)
    input_grad[...] = total
    io.leave(1)
    for k in range(1, 8):
        t, target = line_peer(me, k)
        copy(sums.at[t], grads.at[t], lfs.at[k], lfr.at[t], target).wait_recv()
    square = jnp.zeros((8, 128), F32)
    for t in range(8):
        square = square + fold_squares(grads[t])
    io.leave(2)
    for k in range(1, 8):
        t, target = line_peer(me, k)
        copy(asums.at[t], aland.at[t], las.at[k], lar.at[t], target).wait_recv()
    totals = []
    for side in range(2):
        both = aland[side].astype(F32)
        for t in range(1, 4):
            both = both + aland[side + 2 * t].astype(F32)
        totals.append(jnp.concatenate([both[0:8], both[8:16]], axis=1)[:, 0:ATT])
    eighth = lax.broadcasted_iota(jnp.int32, (8, ATT), 0) == 7
    totals = [totals[0] + jnp.where(eighth, totals[1], 0.0), jnp.where(eighth, 0.0, totals[1])]
    for side in range(2):
        att_grads[side] = totals[side]
        square = square + fold_squares(totals[side])
    io.leave(3)
    squares[0] = square
    lsq[p] = square
    for k in range(1, 8):
        t, target = line_peer(me, k)
        one = copy(squares.at[0], lsq.at[p], qs.at[k], qr.at[p], target)
        one.start()
        sent.append(one)
    for k in range(1, 8):
        t, target = line_peer(me, k)
        copy(squares.at[0], lsq.at[t], qs.at[k], qr.at[t], target).wait_recv()
    line_total = lsq[0]
    for t in range(1, 8):
        line_total = line_total + lsq[t]
    squares[1] = line_total
    psq[q] = line_total
    for k in range(1, 16):
        t, target = plane_peer(me, k)
        one = copy(squares.at[1], psq.at[q], ts.at[k], tr.at[q], target)
        one.start()
        sent.append(one)
    for k in range(1, 16):
        t, target = plane_peer(me, k)
        copy(squares.at[1], psq.at[t], ts.at[k], tr.at[t], target).wait_recv()
    full = psq[0]
    for t in range(1, 16):
        full = full + psq[t]
    norm[...] = full

    @pl.when(core == 1)
    def _():
        give_part(0, 1).wait_send()
        give_part(1, 1).wait_send()

    for one in sent:
        one.wait_send()
    for j in range(2):
        kv_pair(j).wait_send()
        kv_sums[j].drain()
    for ring in nears:
        ring.drain()
    fsum.drain()
    asum.drain()
    for k in range(1, 16):
        t, target = plane_peer(me, k)
        copy(got1.at[t], bland.at[q], bs.at[k], br.at[q], target).wait_send()
    ysum.drain()


def backward(*args):
    row = pltpu.VMEM
    return comm_call(
        backward_kernel,
        (
            shape(TOK, D), shape(TOK, D, dtype=F32), shape(8, 8, FFN, dtype=F32), shape(2, 8, ATT, dtype=F32),
            shape(8, 128, dtype=F32),
        ),
        [
            row((2, TOK // 2, DP), BF), row((2, TOK, DP), BF),
            row((2, 4, 4, 32, D), BF), row((16, 64, 256), BF), row((2, 4, 4, 32, D), BF), row((16, 64, 256), BF),
            row((16, 64, 256), BF), row((16, 8, 128), F32), row((16, 8, 128), F32),
            row((8, 16, 640), BF), row((8, 16, 640), BF), row((8, 8, FFN), F32), row((2, 8, 128), F32),
            row((8, 8, 128), F32), row((16, 8, 128), F32),
            row((2, 8 * TOK, 128), BF), row((TOK, D), BF),
            row((HEADS, TOK, 128), BF), row((8, HD, 2 * TOK), BF), row((8, HD, 2 * TOK), BF),
            row((HEADS, TOK, 128), F32), row((128, 8 * TOK), F32), row((128, 8 * TOK), F32),
            row((2, 2, TOK, 8 * TOK), BF), row((3 * TOK, 8 * TOK), BF),
            row((2, 4, 2, 128, TOK), BF), row((2, 2, 128, TOK), BF), row((2, 2, 2, 128, TOK), BF),
            row((2, 2, 128, TOK), BF), row((2, 128, TOK), BF),
            row((TOK, DP), F32), row((TOK, QKV), BF), row((TOK, DP), F32),
            row((2, 2, 16, 2 * FB), BF), row((2, 2, 32, 2 * FB), BF), dma(2, 6), dma(2, 6),
            *plane_sum_scratch(FB), *plane_sum_scratch(D),
            dma(2), dma(16), dma(16), dma(16), dma(16), dma(6), dma(6), dma(2, 2), dma(2, 2), dma(2, 6), dma(2, 6), dma(2), dma(2),
            dma(8), dma(8), dma(8), dma(8), dma(8), dma(8), dma(16), dma(16),
        ],
        3, *args, far_in=(22,), late=15,
    )


def adam_step(master, first_moment, second_moment, gradient, factor, step_rate, weight_decay):
    clipped = gradient * factor
    first_new = BETA_ONE * first_moment + (1.0 - BETA_ONE) * clipped
    second_new = BETA_TWO * second_moment + (1.0 - BETA_TWO) * clipped * clipped
    direction = (
        first_new
        / (1.0 - BETA_ONE**STEP)
        / (jnp.sqrt(second_new / (1.0 - BETA_TWO**STEP)) + ADAM_EPS)
    )
    master_new = master - step_rate * (direction + weight_decay * master)
    return (master_new, first_new, second_new, master_new.astype(jnp.bfloat16))


def update_kernel(io, squares, grads, att, spread, *refs):
    params, (result_in, input_in) = refs[0:24], refs[24:26]
    outs, (norm, result, input_grad) = refs[26:58], refs[58:61]
    io.arrive()
    result[...] = result_in[...]
    input_grad[...] = input_in[...]
    io.leave(33)
    io.leave(34)
    grad_norm = jnp.sqrt(jnp.sum(jnp.sum(squares[...], axis=0, keepdims=True), axis=1, keepdims=True))
    norm[...] = grad_norm
    factor = CLIP / jnp.maximum(grad_norm, CLIP)

    def step(number, gradient, first, columns):
        lanes = slice(first, first + columns)
        rate = STEP_RATES[number]
        decay = 0.0 if number == 7 else DECAY
        news = adam_step(*(params[3 * number + n][:, lanes] for n in range(3)), gradient, factor, rate, decay)
        for n in range(4):
            outs[4 * number + n][:, lanes] = news[n]

    def done(number):
        for n in range(4):
            io.leave(4 * number + n)

    for n in range(3):
        for t in range(8):
            first, width = (FB * t, FB) if t < 6 else (FB * 6 + 512 * (t - 6), 512)
            start = FB * n
            step(4 + n, grads[t, 0:7, start : start + width], first, width)
        done(4 + n)
    step(0, att[0, 0:7, 0:D], 0, D)
    step(1, att[0, 0:7, D : D + 128], 0, 128)
    step(2, att[0, 0:7, D + 128 : QKV], 0, 128)
    step(7, att[0, 7:8, D : D + NVEC], 0, NVEC)
    for number in (0, 1, 2, 7):
        done(number)
    rest = att[1, :, 0:DP]
    own = jnp.zeros((8, D), F32)
    for _ in range(3):
        part = rest.astype(BF)
        own = own + dot_nt(part, spread[...])
        rest = rest - part.astype(F32)
    step(3, own[0:7], 0, D)


def update(squares, grads, att, spread, params, result, input_grad):
    outs = []
    for number in range(8):
        dims = params[3 * number].shape
        outs += [shape(*dims, dtype=F32)] * 3 + [shape(*dims)]
    outs += [shape(1, 1, dtype=F32), shape(TOK, D), shape(TOK, D, dtype=F32)]
    return comm_call(update_kernel, tuple(outs), [], None, squares, grads, att, spread, *params, result, input_grad)


def per_device(
    tokens, cotangent, layout,
    w_query, m_query, v_query, w_key, m_key, v_key, w_value, m_value, v_value, w_out, m_out, v_out,
    w_gate, m_gate, v_gate, w_up, m_up, v_up, w_down, m_down, v_down, w_vectors, m_vectors, v_vectors,
):
    spread = jnp.asarray(spread_matrix(), BF)
    pick, spots, holds = (jnp.asarray(table, BF) for table in vector_tables())
    turns = jnp.asarray(turn_tables())
    h, n2, o_nat, invp, o_low, vec, cos, sin, n1, x, dy, q_ext, keys, values, wqkv, wo, wdn, wf, dyg, p_far = forward(
        layout, w_query, w_key, w_value, w_vectors[None], w_out, spread, w_gate, w_up, w_down,
        tokens[0], cotangent[0], turns, pick, spots, holds,
    )
    dn2, reduced, y_parts, ffn_grads = feed_forward(n2, wf, dyg, wdn)
    result, input_grad, grads, att, squares = backward(
        reduced, ffn_grads, y_parts, dn2, h, dy, vec, o_low, wo, spread, invp, o_nat, q_ext, keys, values, n1, x, wqkv,
        cos, sin, spots, holds, p_far,
    )
    params = [
        w_query, m_query, v_query, w_key, m_key, v_key, w_value, m_value, v_value, w_out, m_out, v_out,
        w_gate, m_gate, v_gate, w_up, m_up, v_up, w_down, m_down, v_down,
        w_vectors[None], m_vectors[None], v_vectors[None],
    ]
    *news, norm, result, input_grad = update(squares, grads, att, spread, params, result, input_grad)
    return (result[None], input_grad[None], norm[0, 0], *news[:28], *(one[0] for one in news[28:]))


def solution(mesh):
    token_spec = P("fsdp", "ctx", None)
    row_spec = P(("ctx", "fsdp"), None)
    vector_spec = P(("ctx", "fsdp"))
    in_specs = (token_spec, token_spec, P("fsdp", None)) + (row_spec,) * 21 + (vector_spec,) * 3
    out_specs = (token_spec, token_spec, P()) + (row_spec,) * 28 + (vector_spec,) * 4
    return jax.shard_map(
        per_device, mesh=mesh, in_specs=in_specs, out_specs=out_specs, check_vma=False
    )
```

time: 2520 us -> 211 us (0.08)
  blocking collectives: 1410 us -> 0 us
  waiting for transfers between devices: 448 us -> 0 us
  local copies, waits for them, and re-layouts: 255 us -> 0 us
  Pallas kernels: 0 us -> 206 us
  starting transfers between devices: 175 us -> 0 us
  matrix products: 129 us -> 0 us
  other arithmetic: 52.3 us -> 0 us
    unnamed x4 -> x0, blocking collectives: 947 us -> none
    all_gather x5 -> x0, waiting for transfers between devices: 448 us -> none  [the longest x1 193 us: per_device(): lax.all_gather(w_up.astype(jnp.bfloat16), ('ctx', 'fsdp'), axis=0, tiled=...]
    all_gather x4 -> x0, blocking collectives: 401 us -> none  [the longest x1 181 us: per_device(): lax.all_gather(w_value.astype(jnp.bfloat16), ('ctx', 'fsdp'), axis=0, til...]
    unnamed x164 -> x0, local copies, waits for them, and re-layouts: 210 us -> none
    pallas_call x0 -> x4, Pallas kernels: none -> 206 us  [comm_call(): pl.pallas_call(body, out_shape=out_shape, in_specs=[pl.BlockSpec(memory_s...]
    unnamed x49 -> x0, starting transfers between devices: 174 us -> none
    dot_general x49 -> x0, matrix products: 129 us -> none  [the longest x7 32.6 us: outer_sum(): lax.dot_general(left, right, (((0,), (0,)), ((), ())), preferred_element_...]
    psum x1 -> x0, blocking collectives: 63.7 us -> none  [per_device(): square_sum = lax.psum(local_square, ('ctx', 'fsdp'))]
  transfers between devices with their start and end apart: 56 -> 0, of which waited for: 3 -> 0; matrix products, arithmetic and copies ran while one was open for 32% -> 0% of each run, Pallas kernels for 0% -> 0%
where the time goes in v1:
time: 211 us; the launch traced here: 207 us
  Pallas kernels  206 us (98%)
    pallas_call x4, Pallas kernels, comm_call(): pl.pallas_call(body, out_shape=out_shape, in_specs=[pl.BlockSpec(memory_s...  206 us

profile of v1, /device:TPU:1, one launch (start us, length us, event | category | flops | bytes accessed | tf_op | source)
XLA Modules:
  0.0 207.3 jit_solution(14698292892554079541)
XLA Ops:
  0.7 69.7 %shard_map.575 = (f32[256,1024]{1,0:T(8,128)}, bf16[256,1024]{1,0:T(8,128)(2,1)}, f32[256,896]{1,0:T(8,128)}, f32[256,128]{1,0:T(8,128)}, bf16[256,1024]{1,0:T(8...) custom-call(s32[1,32]{1,0:T(1,128)} %refs_0_.1, ...), custom_call_target="tpu_custom_call" | custom-call | tf_op jit(solution)/shard_map/pallas_call | solution.py:468
  70.4 58.5 %shard_map.576 = (f32[256,1024]{1,0:T(8,128)}, bf16[2,4,32,1280]{3,2,1,0:T(8,128)(2,1)}, bf16[4,256,1024]{2,1,0:T(8,128)(2,1)}, bf16[2,4,4,32,640]{4,3,2,1,0:T(8,128)(2,1)}) custom-call(bf16[256,1024]{1,0:T(8,128)(2,1)} %get-tuple-element.99.refs_0_, bf16[2,4,4,32,1280]{4,3,2,1,0:T(8,128)(2,1)} %get-tuple-element.100.refs_1_, ...), custom_call_target="tpu_custom_call" | custom-call | tf_op jit(solution)/shard_map/pallas_call | solution.py:468
  128.9 71.5 %shard_map.577 = (bf16[256,896]{1,0:T(8,128)(2,1)}, f32[256,896]{1,0:T(8,128)}, f32[8,8,1920]{2,1,0:T(8,128)}, f32[2,8,1152]{2,1,0:T(8,128)}, f32[8,128]{1,0:T(8,128)}) custom-call(bf16[2,4,32,1280]{3,2,1,0:T(8,128)(2,1)} %get-tuple-element.103.refs_0_, bf16[2,4,4,32,640]{4,3,2,1,0:T(8,128)(2,1)} %get-tuple-element.104.refs_1_, ...), custom_call_target="tpu_custom_call" | custom-call | tf_op jit(solution)/shard_map/pallas_call | solution.py:468
  200.5 6.5 %shard_map.578 = (f32[7,896]{1,0:T(8,128)}, f32[7,896]{1,0:T(8,128)}, f32[7,896]{1,0:T(8,128)}, bf16[7,896]{1,0:T(8,128)(2,1)}, f32[7,128]{1,0:T(8,128)}, /*inde...) custom-call(f32[8,128]{1,0:T(8,128)} %get-tuple-element.123.refs_0_,, ...), custom_call_target="tpu_custom_call" | custom-call | tf_op jit(solution)/shard_map/pallas_call | solution.py:468

commit v2 on v1

--- a/solution.py
+++ b/solution.py
@@ -836,9 +836,9 @@
 
 
 def ffn_kernel(
-    io, n2, wf, dyg, wdn, dn2_out, reduced, y_far, g_far,
+    io, n2, wf, dyg, wdn, dn2_out, reduced, y_far,
     wd, grads, grads_d, n2g, dparts, yparts, got, tmp, land, hid_all, dgu_all, dhid_all, gu_s,
-    f_tw, f_lw, f_t, f_l, f_s, f_r, leave, wds, wdr, ls, lr, lcs, lcr, gs, gr, ds, dr,
+    f_tw, f_lw, f_t, f_l, f_s, f_r, d_tw, d_lw, d_t, d_l, d_s, d_r, leave, wds, wdr, ls, lr, lcs, lcr, gs, gr, ds, dr,
 ):
     me = place()
     x, y, z, core = me
@@ -954,6 +954,7 @@
     compute(3, after_far)
 
     fsum = PlaneSum(me, grads.at[0], grads.at[1], f_tw, f_lw, f_t, f_l, f_s, f_r)
+    down_sum = PlaneSum(me, grads_d.at[0], grads_d.at[1], d_tw, d_lw, d_t, d_l, d_s, d_r)
     leaves = []
 
     def weight_grads(left, right, into, width, first, last):
@@ -976,8 +977,7 @@
     fsum.wide[1].start()
     dsum.relay()
     weight_grads(dyg, hid_all, grads_d, FB, 0, 4)
-    leaves.append(pltpu.make_async_copy(grads_d, g_far, leave.at[4]))
-    leaves[0].start()
+    down_sum.start()
     fsum.wide[0].relay()
     lax.fori_loop(0, 2, outputs, 0)
     for k in range(2):
@@ -988,6 +988,7 @@
     lax.fori_loop(2, 4, outputs, 0)
     for k in range(2, 4):
         pair(1, yparts, k).start()
+    down_sum.relay_wide()
     for k in range(4):
         join(1, yparts, k)
         t = (z + k) % 4
@@ -995,9 +996,10 @@
         one_out.start()
         leaves.append(one_out)
     for n in range(2):
-        reduced[n] = fsum.wide[n].finish().astype(BF)
+        reduced[n, :, :, 0 : 2 * FB] = fsum.wide[n].finish().astype(BF)
+        reduced[n, :, :, 2 * FB : FFN] = down_sum.wide[n].finish().astype(BF)
     io.leave(1)
-    for ring in fsum.wide + gathers:
+    for ring in fsum.wide + down_sum.wide + gathers:
         ring.drain()
     line.drain()
     for n, ref in enumerate((dparts, yparts)):
@@ -1012,17 +1014,17 @@
     slots = pltpu.VMEM((8, TOK, DP), BF)
     return comm_call(
         ffn_kernel,
-        (shape(TOK, DP, dtype=F32), shape(2, 4, 32, 2 * FB), shape(4, TOK, DP), shape(2, 4, 4, 32, FB)),
+        (shape(TOK, DP, dtype=F32), shape(2, 4, 32, FFN), shape(4, TOK, DP)),
         [
             pltpu.VMEM((2, 4, 4, 32, FB), BF), pltpu.VMEM((2, 4, 4, 32, 2 * FB), BF), pltpu.VMEM((2, 4, 4, 32, FB), BF),
             slots, slots, slots, pltpu.VMEM((2, 4, TOK, DP), BF),
             pltpu.VMEM((2, TOK // 2, DP), BF), pltpu.VMEM((2, TOK, DP), BF),
             pltpu.VMEM((8, TOK, FB), BF), pltpu.VMEM((8, TOK, 2 * FB), BF), pltpu.VMEM((8, TOK, FB), F32),
             pltpu.VMEM((2, TOK, 2 * FB), F32),
-            *plane_sum_scratch(2 * FB), dma(6), dma(2, 6), dma(2, 6),
+            *plane_sum_scratch(2 * FB), *plane_sum_scratch(FB), dma(6), dma(2, 6), dma(2, 6),
             *line_gather_sems(), dma(2, 4), dma(2, 4), dma(6), dma(6),
         ],
-        2, n2, wf, dyg, wdn, far_in=(3,), far_out=(2, 3),
+        2, n2, wf, dyg, wdn, far_in=(3,), far_out=(2,),
     )
 
 
@@ -1041,12 +1043,12 @@
 
 
 def backward_kernel(
-    io, reduced, own, yb, dn2, h, dy, vec, o_low, wb, spread, invp, o_nat, q_ext, k_s, v_in,
+    io, reduced, yb, dn2, h, dy, vec, o_low, wb, spread, invp, o_nat, q_ext, k_s, v_in,
     n1, xs, wa, cos, sin, spots, holds, p_far,
     result, input_grad, grads, att_grads, norm,
     ytmp, yland, ag0, ag1, got0, got1, bland, ent, eland, asums, aland, sums, squares, lsq, psq,
     v_s, do_s, do_ext, do_t, q_t, dq_ext, dkt, dvt, p_s, ds_s, kvp, kvtmp, kvland, give, take, dh, dqkv, dn1,
-    n_t, n_l, n_s, n_r, f_tw, f_lw, f_t, f_l, f_s, f_r, a_tw, a_lw, a_t, a_l, a_s, a_r,
+    n_t, n_l, n_s, n_r, a_tw, a_lw, a_t, a_l, a_s, a_r,
     p_sem, bs, br, es, er, ys, yr, cs, cr, ks, kr, kps, kpr, lfs, lfr, las, lar, qs, qr, ts, tr,
 ):
     me = place()
@@ -1064,10 +1066,9 @@
 
     for unit in range(2):
         get(unit).start()
-    io.start(15)
+    io.start(14)
     greet(line_targets(me) + [plane_peer(me, k)[1] for k in range(1, 16)])
-    io.arrive(3)
-    fsum = PlaneSum(me, own.at[0], own.at[1], f_tw, f_lw, f_t, f_l, f_s, f_r)
+    io.arrive(2)
     asum = PlaneSum(me, got0.at[0], got0.at[1], a_tw, a_lw, a_t, a_l, a_s, a_r)
 
     def send_narrow():
@@ -1095,10 +1096,9 @@
     ]
     for ring in nears:
         ring.start()
-    fsum.start()
     ysum.start()
 
-    io.arrive(10)
+    io.arrive(9)
     scale_two = scale_of(h[...])
     dh_part, dgain_two = norm_back(dn2[...], h[...], scale_two, vec[:, DP : 2 * DP])
     dh[...] = dy[...].astype(F32) + dh_part
@@ -1120,7 +1120,7 @@
 
     do_far = (dot_nt(da[:, 0:A2], wide(wb, 0, 0, A2)) + dot_nt(da[:, A2:DP], wide(wb, 1, 0, A2))).astype(BF)
     do_s[...] = dot_nt(do_far, spread[...]).astype(BF)
-    io.arrive(15)
+    io.arrive(14)
     all_values = v_in[...].reshape(8 * TOK, 128).astype(F32)
     for j in range(2):
         ones = jnp.where(lane(8 * TOK) % HD < 3, 1.0, 0.0)
@@ -1210,7 +1210,6 @@
     kv_sums = [kv_sum(0), kv_sum(1)]
     heads(0)
     heads(1)
-    fsum.relay_wide()
     ysum.relay()
 
     @pl.when(core == 1)
@@ -1221,7 +1220,6 @@
     heads(3)
     kv_pack(0)
     kv_sums[0].start()
-    fsum.narrow()
 
     @pl.when(core == 1)
     def _():
@@ -1230,7 +1228,6 @@
     heads(4)
     heads(5)
     kv_sums[0].relay()
-    fsum.relay()
 
     @pl.when(core == 1)
     def _():
@@ -1311,10 +1308,8 @@
     def _():
         asum.narrow()
 
-    sum_f = fsum.finish()
     for i in range(2):
-        sums[4 * i : 4 * i + 4, :, 0 : 2 * FB] = nears[i].finish().reshape(4, 8, 2 * FB)
-        sums[4 * i : 4 * i + 4, :, 2 * FB : FFN] = sum_f[i].reshape(4, 8, FB)
+        sums[4 * i : 4 * i + 4] = nears[i].finish().reshape(4, 8, FFN)
     for k in range(1, 8):
         t, target = line_peer(me, k)
         one = copy(sums.at[t], grads.at[p], lfs.at[k], lfr.at[p], target)
@@ -1425,7 +1420,6 @@
         kv_sums[j].drain()
     for ring in nears:
         ring.drain()
-    fsum.drain()
     asum.drain()
     for k in range(1, 16):
         t, target = plane_peer(me, k)
@@ -1454,12 +1448,12 @@
             row((2, 4, 2, 128, TOK), BF), row((2, 2, 128, TOK), BF), row((2, 2, 2, 128, TOK), BF),
             row((2, 2, 128, TOK), BF), row((2, 128, TOK), BF),
             row((TOK, DP), F32), row((TOK, QKV), BF), row((TOK, DP), F32),
-            row((2, 2, 16, 2 * FB), BF), row((2, 2, 32, 2 * FB), BF), dma(2, 6), dma(2, 6),
-            *plane_sum_scratch(FB), *plane_sum_scratch(D),
+            row((2, 2, 16, FFN), BF), row((2, 2, 32, FFN), BF), dma(2, 6), dma(2, 6),
+            *plane_sum_scratch(D),
             dma(2), dma(16), dma(16), dma(16), dma(16), dma(6), dma(6), dma(2, 2), dma(2, 2), dma(2, 6), dma(2, 6), dma(2), dma(2),
             dma(8), dma(8), dma(8), dma(8), dma(8), dma(8), dma(16), dma(16),
         ],
-        3, *args, far_in=(22,), late=15,
+        3, *args, far_in=(21,), late=14,
     )
 
 
@@ -1476,16 +1470,18 @@
     return (master_new, first_new, second_new, master_new.astype(jnp.bfloat16))
 
 
-def update_kernel(io, squares, grads, att, spread, *refs):
-    params, (result_in, input_in) = refs[0:24], refs[24:26]
-    outs, (norm, result, input_grad) = refs[26:58], refs[58:61]
-    io.arrive()
+def update_kernel(io, result_in, input_in, squares, grads, att, spread, *refs):
+    params = refs[0:24]
+    outs, (norm, result, input_grad) = refs[24:56], refs[56:59]
+    io.arrive(2)
     result[...] = result_in[...]
+    io.leave(33)
     input_grad[...] = input_in[...]
-    io.leave(33)
     io.leave(34)
+    io.arrive(6)
     grad_norm = jnp.sqrt(jnp.sum(jnp.sum(squares[...], axis=0, keepdims=True), axis=1, keepdims=True))
     norm[...] = grad_norm
+    io.leave(32)
     factor = CLIP / jnp.maximum(grad_norm, CLIP)
 
     def step(number, gradient, first, columns):
@@ -1496,29 +1492,28 @@
         for n in range(4):
             outs[4 * number + n][:, lanes] = news[n]
 
-    def done(number):
-        for n in range(4):
-            io.leave(4 * number + n)
-
-    for n in range(3):
-        for t in range(8):
-            first, width = (FB * t, FB) if t < 6 else (FB * 6 + 512 * (t - 6), 512)
-            start = FB * n
-            step(4 + n, grads[t, 0:7, start : start + width], first, width)
-        done(4 + n)
-    step(0, att[0, 0:7, 0:D], 0, D)
-    step(1, att[0, 0:7, D : D + 128], 0, 128)
-    step(2, att[0, 0:7, D + 128 : QKV], 0, 128)
-    step(7, att[0, 7:8, D : D + NVEC], 0, NVEC)
-    for number in (0, 1, 2, 7):
-        done(number)
     rest = att[1, :, 0:DP]
     own = jnp.zeros((8, D), F32)
     for _ in range(3):
         part = rest.astype(BF)
         own = own + dot_nt(part, spread[...])
         rest = rest - part.astype(F32)
-    step(3, own[0:7], 0, D)
+    blocks = [
+        [(att[0, 0:7, 0:D], 0, D)], [(att[0, 0:7, D : D + 128], 0, 128)], [(att[0, 0:7, D + 128 : QKV], 0, 128)],
+        [(own[0:7], 0, D)],
+    ]
+    spans = [(FB * t, FB) if t < 6 else (FB * 6 + 512 * (t - 6), 512) for t in range(8)]
+    for n in range(3):
+        blocks.append(
+            [(grads[t, 0:7, FB * n : FB * n + width], first, width) for t, (first, width) in enumerate(spans)]
+        )
+    blocks.append([(att[0, 7:8, D : D + NVEC], 0, NVEC)])
+    for number in range(8):
+        io.arrive(9 + 3 * number)
+        for block in blocks[number]:
+            step(number, *block)
+        for n in range(4):
+            io.leave(4 * number + n)
 
 
 def update(squares, grads, att, spread, params, result, input_grad):
@@ -1527,7 +1522,7 @@
         dims = params[3 * number].shape
         outs += [shape(*dims, dtype=F32)] * 3 + [shape(*dims)]
     outs += [shape(1, 1, dtype=F32), shape(TOK, D), shape(TOK, D, dtype=F32)]
-    return comm_call(update_kernel, tuple(outs), [], None, squares, grads, att, spread, *params, result, input_grad)
+    return comm_call(update_kernel, tuple(outs), [], None, result, input_grad, squares, grads, att, spread, *params)
 
 
 def per_device(
@@ -1542,9 +1537,9 @@
         layout, w_query, w_key, w_value, w_vectors[None], w_out, spread, w_gate, w_up, w_down,
         tokens[0], cotangent[0], turns, pick, spots, holds,
     )
-    dn2, reduced, y_parts, ffn_grads = feed_forward(n2, wf, dyg, wdn)
+    dn2, reduced, y_parts = feed_forward(n2, wf, dyg, wdn)
     result, input_grad, grads, att, squares = backward(
-        reduced, ffn_grads, y_parts, dn2, h, dy, vec, o_low, wo, spread, invp, o_nat, q_ext, keys, values, n1, x, wqkv,
+        reduced, y_parts, dn2, h, dy, vec, o_low, wo, spread, invp, o_nat, q_ext, keys, values, n1, x, wqkv,
         cos, sin, spots, holds, p_far,
     )
     params = [

time: 211 us -> 212 us (level)
  no operation moved by 1% of the time
where the time goes in v2:
time: 212 us; the launch traced here: 207 us
  Pallas kernels  206 us (97%)
    pallas_call x4, Pallas kernels, comm_call(): pl.pallas_call(body, out_shape=out_shape, in_specs=[pl.BlockSpec(memory_s...  206 us

profile of v2, /device:TPU:1, one launch (start us, length us, event | category | flops | bytes accessed | tf_op | source)
XLA Modules:
  0.0 207.3 jit_solution(772900757683032704)
XLA Ops:
  0.7 69.8 %shard_map.575 = (f32[256,1024]{1,0:T(8,128)}, bf16[256,1024]{1,0:T(8,128)(2,1)}, f32[256,896]{1,0:T(8,128)}, f32[256,128]{1,0:T(8,128)}, bf16[256,1024]{1,0:T(8...) custom-call(s32[1,32]{1,0:T(1,128)} %refs_0_.1, ...), custom_call_target="tpu_custom_call" | custom-call | tf_op jit(solution)/shard_map/pallas_call | solution.py:468
  70.4 62.9 %shard_map.576 = (f32[256,1024]{1,0:T(8,128)}, bf16[2,4,32,1920]{3,2,1,0:T(8,128)(2,1)}, bf16[4,256,1024]{2,1,0:T(8,128)(2,1)}) custom-call(bf16[256,1024]{1,0:T(8,128)(2,1)} %get-tuple-element.98.refs_0_, bf16[2,4,4,32,1280]{4,3,2,1,0:T(8,128)(2,1)} %get-tuple-element.99.refs_1_, bf16[8,256,1024]{2,1,0:T(8,128)(2,1)} %get-tuple-element.100.refs_2_, ...), custom_call_target="tpu_custom_call" | custom-call | tf_op jit(solution)/shard_map/pallas_call | solution.py:468
  133.4 67.8 %shard_map.577 = (bf16[256,896]{1,0:T(8,128)(2,1)}, f32[256,896]{1,0:T(8,128)}, f32[8,8,1920]{2,1,0:T(8,128)}, f32[2,8,1152]{2,1,0:T(8,128)}, f32[8,128]{1,0:T(8,128)}) custom-call(bf16[2,4,32,1920]{3,2,1,0:T(8,128)(2,1)} %get-tuple-element.102.refs_0_, bf16[4,256,1024]{2,1,0:T(8,128)(2,1)} %get-tuple-element.103.refs_1_, ...), custom_call_target="tpu_custom_call" | custom-call | tf_op jit(solution)/shard_map/pallas_call | solution.py:468
  201.2 5.8 %shard_map.578 = (f32[7,896]{1,0:T(8,128)}, f32[7,896]{1,0:T(8,128)}, f32[7,896]{1,0:T(8,128)}, bf16[7,896]{1,0:T(8,128)(2,1)}, f32[7,128]{1,0:T(8,128)}, /*inde...) custom-call(bf16[256,896]{1,0:T(8,128)(2,1)} %get-tuple-element.121., ...), custom_call_target="tpu_custom_call" | custom-call | tf_op jit(solution)/shard_map/pallas_call | solution.py:468
